TPU v7x, 512 devices: a whole 4x4x16 slice. The times are simulated.
512 devices in a mesh: gx: 4 (over x), gy: 4 (over y), gz: 32 (over z, core).
Axes of the slice: x: 4, y: 4, z: 16, core: 2. Of those that a mesh axis runs over, the one named last changes fastest.
Arguments:
- substrate: float32 [128, 128, 512], P('gz', 'gx', 'gy'), may hold values from 0 to 2
- oxygen: float32 [128, 128, 512], P('gz', 'gx', 'gy'), may hold values from 0 to 1
- velocity: float32 [3, 128, 128, 512], P(None, 'gz', 'gx', 'gy'), may hold values from -0.2 to 0.2
- cell_map: int32 [128, 128, 512], P('gz', 'gx', 'gy'), may hold values from 0 to 8191, as said below
- owner_slot: int32 [8192], replicated, may hold values from 0 to 15871, as said below
- flow_list: int32 [2, 8192], replicated, may hold values from 0 to 8191, as said below
- flow_rates: float32 [16], replicated, may hold values from 0.05 to 0.4
- population: float32 [15872, 64, 256], P(('gx', 'gy', 'gz')), may hold values from 0.05 to 1
- growth: bfloat16 [256, 256], replicated, may hold values from -1 to 1
- daughter_kernel: bfloat16 [256, 256], replicated, may hold values from -1 to 1
- division_rate: float32 [64, 256], replicated, may hold values from 0.02 to 0.6
- uptake_weight: float32 [2, 256], replicated, may hold values from 0.1 to 1
Outputs:
- substrate_out: float32 [128, 128, 512], P('gz', 'gx', 'gy')
- oxygen_out: float32 [128, 128, 512], P('gz', 'gx', 'gy')
- population_out: float32 [15872, 64, 256], P(('gx', 'gy', 'gz'))
Inputs may be any that keep to these rules, and one draw needn't show every extreme that they name: `cell_map`: every compartment holds exactly 1024 cells. `owner_slot`: distinct slots. The device with index d along gx+gy+gz holds slots d * 31 to d * 31 + 30, and its compartments fill a leading run of them, one at least. Two devices whose gz indices differ only in the lowest bit hold 32 compartments together. Some device holds 31. `flow_list`: A flow's target is owned by a device with the same gz index as its source's owner. From one device at most 2 flows go to the compartments of any one device, and some device sends 2 to some device.
All inputs are finite; a program needn't handle non-finite values.
Results may differ from a plain program's by a relative error of at most 0.0015.
The roundings to bfloat16 on the way count: a program that leaves them out, or rounds other values in their place, can miss the bound.
Values sent between devices are 32-bit elements; how exact they have to be, the bound alone decides.
A program may use at most 64 MiB of HBM per device.

v0:
```python
import jax
import jax.numpy as jnp
from jax import lax
from jax.sharding import PartitionSpec as P

SUBSTEPS = 8
CELLS = 1024


diffusion = 0.05
growth_max = 0.8
half_substrate = 0.3
half_oxygen = 0.1
uptake_gain = 3.0


def padded_2(block, sides, width):
    for axis, dim in sides:
        count = lax.axis_size(axis)
        forward = [(i, i + 1) for i in range(count - 1)]
        backward = [(target, source) for source, target in forward]
        low = lax.ppermute(
            lax.slice_in_dim(block, block.shape[dim] - width, None, axis=dim), axis, forward
        )
        high = lax.ppermute(lax.slice_in_dim(block, 0, width, axis=dim), axis, backward)
        block = jnp.concatenate([low, block, high], axis=dim)
    return block


def stencil(padded, velocity):
    center = padded[:, 1:-1, 1:-1, 1:-1]
    lower_side = [
        padded[:, :-2, 1:-1, 1:-1],
        padded[:, 1:-1, :-2, 1:-1],
        padded[:, 1:-1, 1:-1, :-2],
    ]
    upper_side = [padded[:, 2:, 1:-1, 1:-1], padded[:, 1:-1, 2:, 1:-1], padded[:, 1:-1, 1:-1, 2:]]
    total_change = center
    for axis_id in range(3):
        courant = velocity[axis_id][None]
        total_change = total_change + diffusion * (
            lower_side[axis_id] + upper_side[axis_id] - 2.0 * center
        )
        total_change = total_change - jnp.maximum(courant, 0.0) * (center - lower_side[axis_id])
        total_change = total_change - jnp.minimum(courant, 0.0) * (upper_side[axis_id] - center)
    return total_change


def grow(block_pop, rate_block, growth, daughter_kernel, division_rate):
    rate_scale = rate_block[:, None, None]
    age_bins = block_pop.shape[1]
    for substep in range(SUBSTEPS):
        moved_pop = jnp.einsum(
            "mas,st->mat",
            block_pop.astype(jnp.bfloat16),
            growth,
            preferred_element_type=jnp.float32,
        )
        grown_pop = block_pop + rate_scale * (moved_pop - block_pop)
        split_pop = division_rate[None] * rate_scale * grown_pop
        remain = grown_pop - split_pop
        mothers = jnp.sum(split_pop, axis=1).astype(jnp.bfloat16)
        newborn = 2.0 * jnp.dot(mothers, daughter_kernel, preferred_element_type=jnp.float32)
        oldest = remain[:, age_bins - 2] + remain[:, age_bins - 1]
        block_pop = jnp.concatenate(
            [newborn[:, None], remain[:, : age_bins - 2], oldest[:, None]], axis=1
        )
    return block_pop


def per_device(
    substrate,
    oxygen,
    velocity,
    cell_map,
    owner_slot,
    flow_list,
    flow_rates,
    population,
    growth,
    daughter_kernel,
    division_rate,
    uptake_weight,
):
    fields = jnp.stack([substrate, oxygen])
    padded = padded_2(fields, (("gx", 2), ("gy", 3), ("gz", 1)), 1)
    swept_fields = stencil(padded, velocity)
    count_all = owner_slot.shape[0]
    slot_count = population.shape[0]
    age_bins = population.shape[1]
    size_bins = population.shape[2]
    flat_map = cell_map.reshape(-1)
    partial_value = jnp.stack(
        [
            jax.ops.segment_sum(swept_fields[index].reshape(-1), flat_map, num_segments=count_all)
            for index in range(2)
        ]
    )
    first_slot = lax.axis_index(("gx", "gy", "gz")) * slot_count
    slot_iota = jnp.arange(slot_count, dtype=jnp.int32)
    owned_table = owner_slot[None, :] == (first_slot + slot_iota)[:, None]
    owned_float = owned_table.astype(jnp.float32)
    biomass_slot = jnp.einsum(
        "kas,js->jk", population, uptake_weight, precision=lax.Precision.HIGHEST
    ) / (age_bins * size_bins)
    biomass_own = jnp.dot(biomass_slot, owned_float, precision=lax.Precision.HIGHEST)
    field_sums, biomass = lax.psum((partial_value, biomass_own), ("gx", "gy", "gz"))
    means_all = field_sums / CELLS
    rate_all = (
        growth_max
        * means_all[0]
        / (half_substrate + means_all[0])
        * means_all[1]
        / (half_oxygen + means_all[1])
    )
    uptake = uptake_gain * rate_all[None] * biomass
    halves = jnp.array([half_substrate, half_oxygen], dtype=jnp.float32)[:, None, None, None]
    drawn_cells = uptake[:, cell_map]
    fields_out = swept_fields - drawn_cells * swept_fields / (halves + swept_fields)
    occupied = jnp.any(owned_table, axis=1)
    rate_slot = jnp.dot(owned_float, rate_all, precision=lax.Precision.HIGHEST)
    result = grow(population, rate_slot, growth, daughter_kernel, division_rate)
    comp_iota = jnp.arange(count_all, dtype=jnp.int32)
    slot_comp = jnp.sum(jnp.where(owned_table, comp_iota[None, :], 0), axis=1)
    target = flow_list[0][slot_comp]
    rate_index = flow_list[1][slot_comp]
    outflow_scale = jnp.where(occupied, flow_rates[rate_index], 0.0)
    outflow = result * outflow_scale[:, None, None]
    target_slot = owner_slot[target]
    depth_count = lax.axis_size("gz")
    row_count = lax.axis_size("gx")
    col_count = lax.axis_size("gy")
    columns = row_count * col_count
    destination = target_slot // slot_count // depth_count
    local_slot = target_slot % slot_count
    earlier = (
        (destination[None, :] == destination[:, None])
        & occupied[None, :]
        & (slot_iota[None, :] < slot_iota[:, None])
    )
    rank_within = jnp.sum(earlier.astype(jnp.int32), axis=1)
    place_index = jnp.where(occupied, destination * 2 + rank_within, -1)
    hit_table = place_index[None, :] == jnp.arange(2 * columns, dtype=jnp.int32)[:, None]
    filled = jnp.any(hit_table, axis=1)
    picked = jnp.sum(jnp.where(hit_table, slot_iota[None, :], 0), axis=1)
    flat_out = outflow.reshape(slot_count, age_bins * size_bins)
    payload = jnp.where(filled[:, None], flat_out[picked], 0.0)
    tag_slots = jnp.where(filled, local_slot[picked], -1)
    incoming, mark_slots = (
        lax.all_to_all(
            payload.reshape(columns, 2, age_bins * size_bins),
            ("gx", "gy"),
            split_axis=0,
            concat_axis=0,
            tiled=True,
        ),
        lax.all_to_all(
            tag_slots.reshape(columns, 2), ("gx", "gy"), split_axis=0, concat_axis=0, tiled=True
        ),
    )
    incoming = incoming.reshape(2 * columns, age_bins * size_bins)
    mark_slots = mark_slots.reshape(2 * columns)
    into_table = (mark_slots[None, :] == slot_iota[:, None]).astype(jnp.float32)
    inflow = jnp.dot(into_table, incoming, precision=lax.Precision.HIGHEST).reshape(
        slot_count, age_bins, size_bins
    )
    final_pop = jnp.where(occupied[:, None, None], result - outflow + inflow, 0.0)
    return (fields_out[0], fields_out[1], final_pop)


def solution(mesh):
    return jax.shard_map(
        per_device,
        mesh=mesh,
        in_specs=(
            P("gz", "gx", "gy"),
            P("gz", "gx", "gy"),
            P(None, "gz", "gx", "gy"),
            P("gz", "gx", "gy"),
            P(),
            P(),
            P(),
            P(("gx", "gy", "gz"), None, None),
            P(),
            P(),
            P(),
            P(),
        ),
        out_specs=(P("gz", "gx", "gy"), P("gz", "gx", "gy"), P(("gx", "gy", "gz"), None, None)),
        check_vma=False,
    )
```

profile of v0, /device:TPU:1, one launch (start us, length us, event | category | flops | bytes accessed | tf_op | source)
XLA Modules:
  0.0 807.5 jit_solution(3219477372704684865)
XLA Ops:
  8.1 1.3 collective-permute-start.1
  9.4 4.6 collective-permute-start
  17.9 1.5 gather_fusion.4
  21.3 7.0 all-to-all-start
  28.9 1.1 fusion.23
  30.9 3.2 collective-permute-start.2
  34.1 1.3 collective-permute-start.3
  36.4 3.8 collective-permute-done.3
  40.4 6.7 collective-permute-start.4
  47.0 2.0 collective-permute-start.5
  49.1 1.3 gather_fusion.2
  50.3 2.4 collective-permute-done.5
  53.1 95.2 %scatter_custom_fusion.1 = f32[8192]{0:T(1024)S(1)} fusion(s32[16384]{0:T(1024)} %bitcast.165, f32[16384]{0:T(1024)S(1)} %bitcast.168, f32[]{:T(128)} %constant.28.clone.1), kind=kCustom, calls=%fused_computation.188 | custom fusion | flops 16384 | bytes 33280 | tf_op jit(solution)/shard_map/scatter-add | solution.py:95
  148.3 95.3 %scatter_custom_fusion = f32[8192]{0:T(1024)S(1)} fusion(s32[16384]{0:T(1024)} %bitcast.166, f32[16384]{0:T(1024)S(1)} %bitcast.167, f32[]{:T(128)} %constant.28.clone.1), kind=kCustom, calls=%fused_computation.190 | custom fusion | flops 16384 | bytes 33280 | tf_op jit(solution)/shard_map/scatter-add | solution.py:95
  246.3 1.4 reduce.3
  248.3 449.7 %all-reduce.3.cloned.1.call-done = (f32[2,8192]{1,0:T(2,128)}, f32[2,8192]{1,0:T(2,128)}) async-done(((f32[2,8192]{1,0:T(2,128)}, f32[2,8192]{1,0:T(2,128)}), (f32[2,8192]{1,0:T(2,128)}, f32[2,8192]{1,0:T(2,128)})) %all-reduce.3.cloned.1.call-update) | async-done | bytes 131088 | tf_op jit(solution)/shard_map/psum | solution.py:107
  699.0 1.2 fusion.46
  700.2 1.7 fusion.1
  702.2 1.1 fusion.3
  703.5 1.1 fusion.5
  706.2 1.1 fusion.9
  713.2 1.2 copy.62
  714.6 2.8 gather_fusion.6
  717.4 2.5 gather.36
  719.9 2.5 broadcast_select_fusion
  722.4 4.4 all-to-all-start.1
  726.8 2.6 copy.49
  729.5 56.6 %gather_fusion = f32[16384,2]{1,0:T(8,128)} fusion(f32[2,8192]{0,1:T(8,128)} %copy.49, s32[16384]{0:T(1024)S(1)} %broadcast_clamp_fusion), kind=kCustom, calls=%fused_computation | custom fusion | bytes 327680 | tf_op jit(solution)/shard_map/gather | solution.py:118
  786.1 5.2 copy.50
  792.4 2.5 reshape.183
  794.8 2.8 fusion.16
  797.7 3.0 fusion.20
  (124 shorter events, 22.7 us)
Async XLA Ops:
  7.2 693.1 %copy-start = (bf16[256,256]{1,0:T(8,128)(2,1)S(1)}, bf16[256,256]{1,0:T(8,128)(2,1)}, u32[]{:S(2)}) copy-start(bf16[256,256]{1,0:T(8,128)(2,1)} %param.21) | copy-start | bytes 393220
  7.2 21.2 %copy-start.9 = (f32[3,4,32,128]{3,2,1,0:T(8,128)S(1)}, f32[3,4,32,128]{3,2,1,0:T(8,128)}, u32[]{:S(2)}) copy-start(f32[3,4,32,128]{3,2,1,0:T(8,128)} %param.15) | copy-start | bytes 589828
  7.2 21.3 %copy-start.11 = (s32[4,32,128]{2,1,0:T(8,128)S(1)}, s32[4,32,128]{2,1,0:T(8,128)}, u32[]{:S(2)}) copy-start(s32[4,32,128]{2,1,0:T(8,128)} %param.16) | copy-start | bytes 196612
  7.2 21.3 %copy-start.6 = (f32[31,64,256]{2,1,0:T(8,128)S(1)}, f32[31,64,256]{2,1,0:T(8,128)}, u32[]{:S(2)}) copy-start(f32[31,64,256]{2,1,0:T(8,128)} %param.20) | copy-start | bytes 6094852
  8.1 22.6 %collective-permute-start.1 = (f32[2,4,1,128]{3,2,1,0:T(1,128)S(1)}, f32[2,4,1,128]{3,2,1,0:T(1,128)S(1)}, u32[]{:S(2)}, u32[]{:S(2)}) collective-permute-start(f32[2,4,1,128]{3,2,1,0:T(1,128)S(1)} %get-tuple-element.38), channel_id=1, source_target_pairs={{128,0},{256,128},{384,256},{129,1},{257,129},{385,257},{130,2},{2... | collective-permute-start | bytes 12296 | tf_op jit(solution)/shard_map/ppermute | solution.py:25
  9.4 21.3 %collective-permute-start = (f32[2,4,1,128]{3,2,1,0:T(1,128)S(1)}, f32[2,4,1,128]{3,2,1,0:T(1,128)S(1)}, u32[]{:S(2)}, u32[]{:S(2)}) collective-permute-start(f32[2,4,1,128]{3,2,1,0:T(1,128)S(1)} %get-tuple-element.37), channel_id=1, source_target_pairs={{0,128},{128,256},{256,384},{1,129},{129,257},{257,385},{2,130},{1... | collective-permute-start | bytes 12296 | tf_op jit(solution)/shard_map/ppermute | solution.py:22
  14.0 14.9 %copy-start.16 = (s32[31]{0:T(128)}, s32[31]{0:T(128)S(1)}, u32[]{:S(2)}) copy-start(s32[31]{0:T(128)S(1)} %iota_add_fusion) | copy-start | bytes 376
  17.8 10.9 %copy-start.18 = (f32[2,256]{1,0:T(2,128)S(1)}, f32[2,256]{1,0:T(2,128)}, u32[]{:S(2)}) copy-start(f32[2,256]{1,0:T(2,128)} %param.24) | copy-start | bytes 6148
  17.8 11.1 %copy-start.2 = (s32[8192]{0:T(1024)S(1)}, s32[8192]{0:T(1024)}, u32[]{:S(2)}) copy-start(s32[8192]{0:T(1024)} %param.17) | copy-start | bytes 98308
  19.8 10.9 %copy-start.20 = (pred[32]{0:T(512)(128)(4,1)}, pred[32]{0:T(512)(128)(4,1)S(1)}, u32[]{:S(2)}) copy-start(pred[32]{0:T(512)(128)(4,1)S(1)} %fusion.74) | copy-start | bytes 100
  19.9 10.9 %copy-start.13 = (s32[1024]{0:T(1024)}, s32[1024]{0:T(1024)S(1)}, u32[]{:S(2)}) copy-start(s32[1024]{0:T(1024)S(1)} %pad_clamp_fusion) | copy-start | bytes 12292
  19.9 10.9 %copy-start.7 = (f32[4,32,128]{2,1,0:T(8,128)S(1)}, f32[4,32,128]{2,1,0:T(8,128)}, u32[]{:S(2)}) copy-start(f32[4,32,128]{2,1,0:T(8,128)} %param.13) | copy-start | bytes 196612
  19.9 10.9 %copy-start.8 = (f32[4,32,128]{2,1,0:T(8,128)S(1)}, f32[4,32,128]{2,1,0:T(8,128)}, u32[]{:S(2)}) copy-start(f32[4,32,128]{2,1,0:T(8,128)} %param.14) | copy-start | bytes 196612
  21.3 224.4 %all-to-all-start = ((s32[16,1,2]{2,1,0:T(1,128)}), s32[16,1,2]{2,1,0:T(1,128)}, u32[]{:S(2)}, u32[]{:S(2)}) async-start(s32[16,1,2]{2,1,0:T(1,128)} %bitcast.40), calls=%async_computation | async-start | bytes 16384 | tf_op jit(solution)/shard_map/all_to_all | solution.py:157
  28.4 669.6 %all-reduce.3.cloned.1.call-start = ((), (), s32[]{:S(2)}) async-start(), calls=%async_computation.2 | async-start | bytes 262144 | tf_op jit(solution)/shard_map/psum | solution.py:107
  28.5 20.5 %copy-start.1 = (f32[16]{0:T(128)S(1)}, f32[16]{0:T(128)}, u32[]{:S(2)}) copy-start(f32[16]{0:T(128)} %param.19) | copy-start | bytes 196
  30.9 5.5 collective-permute-start.2
  34.1 6.1 collective-permute-start.3
  40.4 10.0 %collective-permute-start.4 = (f32[2,1,34,130]{3,2,1,0:T(8,128)S(1)}, f32[2,1,34,130]{3,2,1,0:T(8,128)S(1)}, u32[]{:S(2)}, u32[]{:S(2)}) collective-permute-start(f32[2,1,34,130]{3,2,1,0:T(8,128)S(1)} %get-tuple-element.24), channel_id=1, source_target_pairs={{0,1},{1,2},{2,3},{3,4},{4,5},{5,6},{6,7},{7,8},{8,9},{9,10},{10,1... | collective-permute-start | bytes 106088 | tf_op jit(solution)/shard_map/ppermute | solution.py:22
  47.0 5.8 collective-permute-start.5
  245.0 469.4 %copy-start.14 = (f32[31]{0:T(128)}, f32[31]{0:T(128)S(1)}, u32[]{:S(2)}) copy-start(f32[31]{0:T(128)S(1)} %broadcast_select_fusion.2) | copy-start | bytes 376
  700.2 1.8 copy-start.3
  700.2 2.0 copy-start.10
  711.3 1.3 copy-start.4
  722.4 4.4 copy-start.12
  722.4 69.9 %all-to-all-start.1 = ((f32[16,2,16384]{2,1,0:T(2,128)}), f32[16,2,16384]{2,1,0:T(2,128)S(1)}, u32[]{:S(2)}, u32[]{:S(2)}) async-start(f32[16,2,16384]{2,1,0:T(2,128)} %broadcast_select_fusion), calls=%async_computation.1 | async-start | bytes 4194304 | tf_op jit(solution)/shard_map/all_to_all | solution.py:150
  786.1 5.2 copy-start.19
  792.3 2.5 copy-start.17
  794.8 2.9 copy-start.5
  794.8 2.9 copy-start.15
Sparse Core Ops, SparseCore 0:
  244.5 453.4 all-reduce.2
where the time goes:
time: 808 us
  waiting for transfers between devices  457 us (57%)
  other arithmetic  205 us (25%)
  local copies, waits for them, and re-layouts  84.4 us (10%)
  starting transfers between devices  30.5 us (4%)
  matrix products  15.7 us (2%)
  between operations  14.8 us (2%)
    psum x1, waiting for transfers between devices, per_device(): lax.psum((partial_value, biomass_own), ('gx', 'gy', 'gz'))  450 us
    scatter-add x2, other arithmetic, per_device(): jax.ops.segment_sum(swept_fields[index].reshape(-1), flat_map, num_segmen...  190 us
    gather x2, local copies, waits for them, and re-layouts, per_device(): drawn_cells = uptake[:, cell_map]  61.8 us
  transfers between devices with their start and end apart: 9, of which 4 were waited for; matrix products, arithmetic and copies ran while one was open for 34% of the time, Pallas kernels for 0%

commit v1 on v0

v1 whole, which is shorter than its diff:
```python
import functools

import jax
import jax.numpy as jnp
from jax import lax
from jax.experimental import pallas as pl
from jax.experimental.pallas import tpu as pltpu
from jax.sharding import PartitionSpec as P

SUBSTEPS = 8
CELLS = 1024
SLOTS = 31
AGES = 64
SIZES = 256
COLS = 16
DEPTH = 32
LANES = 128
GROUP = 8
NONE_KEY = 65536.0

diffusion = 0.05
growth_max = 0.8
half_substrate = 0.3
half_oxygen = 0.1
uptake_gain = 3.0

MESH = pl.DeviceIdType.MESH
VMEM_SPEC = pl.BlockSpec(memory_space=pltpu.VMEM)
SMEM_SPEC = pl.BlockSpec(memory_space=pltpu.SMEM)
ANY_SPEC = pl.BlockSpec(memory_space=pl.ANY)
VMEM_BYTES = 48 * 1024 * 1024


def iota(shape, dim):
    return lax.broadcasted_iota(jnp.int32, shape, dim)


def device_of(slot):
    return (slot * 33826) >> 20


def lookup(table_row, index, high, row_id, total):
    row = jnp.broadcast_to(table_row, index.shape)
    found = jnp.take_along_axis(row, index, axis=1)
    return jnp.where(high == row_id, found, total)


def prepare_kernel(
    owner_ref,
    flow_ref,
    map_ref,
    weight_ref,
    pop_ref,
    pos_ref,
    bio_ref,
    list_ref,
    payload_ref,
    pop_vmem,
    target_ref,
    index_ref,
    place_ref,
    row_ref,
    ages_ref,
    list_smem,
    pop_sem,
    list_sem,
    pay_sem,
):
    column = lax.axis_index("gx") * 4 + lax.axis_index("gy")
    depth = lax.axis_index("gz")
    me = column * DEPTH + depth
    load = pltpu.make_async_copy(pop_ref, pop_vmem.at[pl.ds(0, SLOTS)], pop_sem)
    load.start()
    for row in range(64):
        lanes = slice(row * LANES, (row + 1) * LANES)
        target_ref[row : row + 1, :] = flow_ref[0:1, lanes]
        index_ref[row : row + 1, :] = flow_ref[1:2, lanes]

    owner = owner_ref[...]
    targets = target_ref[...]
    low, high = targets & 127, targets >> 7
    target_slot = jnp.zeros_like(owner)
    for row in range(64):
        target_slot = lookup(owner_ref[row : row + 1, :], low, high, row, target_slot)
    rate_index = index_ref[...]
    source_dev = device_of(owner)
    source_local = owner - source_dev * SLOTS
    target_dev = device_of(target_slot)
    target_local = target_slot - target_dev * SLOTS
    send_key = (source_local * 16 + rate_index).astype(jnp.float32)
    recv_key = (source_local * 512 + target_local * 16 + rate_index).astype(jnp.float32)
    send_col = jnp.where(source_dev == me, target_dev >> 5, -1)
    recv_col = jnp.where(target_dev == me, source_dev >> 5, -1)
    for col in range(COLS):
        for kind, (key, cols) in enumerate(((send_key, send_col), (recv_key, recv_col))):
            hit = cols == col
            low_row = jnp.min(jnp.where(hit, key, NONE_KEY), axis=0, keepdims=True)
            high_row = jnp.max(jnp.where(hit, key, -1.0), axis=0, keepdims=True)
            at = kind * 32 + col
            row_ref[at : at + 1, :] = low_row
            row_ref[at + 16 : at + 17, :] = high_row
    square = (64, LANES)
    rows = row_ref[...]
    is_low = (iota((64, 1), 0) & 16) == 0
    reduced = jnp.where(
        is_low, jnp.min(rows, axis=1, keepdims=True), jnp.max(rows, axis=1, keepdims=True)
    )
    diagonal = jnp.where(iota(square, 0) == iota(square, 1), reduced, 0.0)
    list_ref[...] = jnp.sum(diagonal, axis=0, keepdims=True).astype(jnp.int32)
    to_scalar = pltpu.make_async_copy(list_ref, list_smem, list_sem)
    to_scalar.start()
    owned = jnp.where(source_dev == me, 1.0, 0.0)
    held = jnp.sum(jnp.sum(owned, axis=0, keepdims=True), axis=1, keepdims=True)

    load.wait()
    to_scalar.wait()
    for col in range(COLS):
        lowest, highest = list_smem[0, col], list_smem[0, col + 16]
        first = jnp.where(highest >= 0, lowest >> 4, 0)
        second = jnp.where(highest >= 0, highest >> 4, 0)
        for rank, slot in enumerate((first, second)):
            pltpu.make_async_copy(
                pop_vmem.at[slot],
                payload_ref.at[col, pl.ds(rank * AGES, AGES)],
                pay_sem.at[col * 2 + rank],
            ).start()

    core = source_dev & 1
    place_ref[...] = (source_dev >> 1) * 32 + jnp.where(core == 1, 31 - source_local, source_local)
    cells = map_ref[...].reshape(LANES, LANES)
    low, high = cells & 127, cells >> 7

    def find(step, total):
        for part in range(8):
            row = step * 8 + part
            total = lookup(place_ref[pl.ds(row, 1), :], low, high, row, total)
        return total

    place = lax.fori_loop(0, 8, find, jnp.zeros_like(cells))
    pos_ref[...] = place.reshape(pos_ref.shape)

    for slot in range(SLOTS):
        ages_ref[slot : slot + 1, :] = jnp.sum(pop_vmem[slot], axis=0, keepdims=True)
    ages_ref[SLOTS : SLOTS + 1, :] = jnp.zeros((1, SIZES), jnp.float32)
    summed = ages_ref[...]
    block = (depth >> 1) & 3
    wide = (32, LANES)
    lane = iota(wide, 1)
    local = lane & 31
    slot_of_lane = jnp.where((depth & 1) == 1, 31 - local, local)
    here = ((lane >> 5) == block) & (slot_of_lane == iota(wide, 0))
    here = here & (slot_of_lane.astype(jnp.float32) < held)
    for field in range(2):
        weighted = summed * weight_ref[field : field + 1, :]
        mass = jnp.sum(weighted, axis=1, keepdims=True) / (AGES * SIZES)
        bio_ref[field : field + 1, :] = jnp.sum(
            jnp.where(here, mass, 0.0), axis=0, keepdims=True
        )
    bio_ref[2:3, :] = jnp.sum(jnp.where(here, 1.0, 0.0), axis=0, keepdims=True)
    bio_ref[3:8, :] = jnp.zeros((5, LANES), jnp.float32)

    for item in range(2 * COLS):
        pltpu.make_async_copy(
            pop_vmem.at[0],
            payload_ref.at[item // 2, pl.ds((item % 2) * AGES, AGES)],
            pay_sem.at[item],
        ).wait()


def prepare(owner, flow, cell_map, weight, population):
    return pl.pallas_call(
        prepare_kernel,
        out_shape=(
            jax.ShapeDtypeStruct(cell_map.shape, jnp.int32),
            jax.ShapeDtypeStruct((8, LANES), jnp.float32),
            jax.ShapeDtypeStruct((1, LANES), jnp.int32),
            jax.ShapeDtypeStruct((COLS, 2 * AGES, SIZES), jnp.float32),
        ),
        in_specs=[VMEM_SPEC, VMEM_SPEC, VMEM_SPEC, VMEM_SPEC, ANY_SPEC],
        out_specs=(VMEM_SPEC, VMEM_SPEC, VMEM_SPEC, ANY_SPEC),
        scratch_shapes=[
            pltpu.VMEM((32, AGES, SIZES), jnp.float32),
            pltpu.VMEM((64, LANES), jnp.int32),
            pltpu.VMEM((64, LANES), jnp.int32),
            pltpu.VMEM((64, LANES), jnp.int32),
            pltpu.VMEM((64, LANES), jnp.float32),
            pltpu.VMEM((32, SIZES), jnp.float32),
            pltpu.SMEM((1, LANES), jnp.int32),
            pltpu.SemaphoreType.DMA,
            pltpu.SemaphoreType.DMA,
            pltpu.SemaphoreType.DMA((2 * COLS,)),
        ],
        compiler_params=pltpu.CompilerParams(vmem_limit_bytes=VMEM_BYTES),
        cost_estimate=pl.CostEstimate(flops=8_000_000, bytes_accessed=6_000_000, transcendentals=0),
    )(owner, flow, cell_map, weight, population)


def sweep_kernel(
    sub_ref,
    oxy_ref,
    vel_ref,
    pos_ref,
    bio_ref,
    swept_ref,
    table_ref,
    x_send,
    x_recv,
    y_send,
    y_recv,
    z_recv,
    value_ref,
    sums_ref,
    a_recv,
    b_send,
    b_recv,
    c_send,
    c_recv,
    d_send,
    d_recv,
    halo_send_sem,
    halo_recv_sem,
    send_sem,
    recv_sem,
):
    gx, gy, gz = lax.axis_index("gx"), lax.axis_index("gy"), lax.axis_index("gz")
    column = gx * 4 + gy
    col_peers = [lax.rem(column + step, COLS) for step in range(1, COLS)]
    deep_peers = [lax.rem(gz + step, DEPTH) for step in range(1, DEPTH)]
    col_ids = [(peer // 4, lax.rem(peer, 4), gz) for peer in col_peers]
    deep_ids = [(gx, gy, peer) for peer in deep_peers]

    barrier = pltpu.get_barrier_semaphore()
    for peer in col_ids + deep_ids:
        pl.semaphore_signal(barrier, inc=1, device_id=peer, device_id_type=MESH)

    fields = (sub_ref, oxy_ref)
    for field, ref in enumerate(fields):
        layers = slice(field * 4, field * 4 + 4)
        x_send[0, layers, :] = ref[:, 0, :]
        x_send[1, layers, :] = ref[:, 31, :]
        turned = ref[...].reshape(LANES, LANES).T
        y_send[0, field : field + 1, :] = turned[0:1, :]
        y_send[1, field : field + 1, :] = turned[LANES - 1 : LANES, :]
    pl.semaphore_wait(barrier, len(col_ids) + len(deep_ids))

    halos = []
    for side in range(2):
        step = 3 if side == 0 else 1
        near_x = (lax.rem(gx + step, 4), gy, gz)
        near_y = (gx, lax.rem(gy + step, 4), gz)
        near_z = (gx, gy, lax.rem(gz + (DEPTH - 1 if side == 0 else 1), DEPTH))
        layer = 0 if side == 0 else 3
        pairs = [
            (x_send.at[side], x_recv.at[1 - side], near_x),
            (y_send.at[side], y_recv.at[1 - side], near_y),
            (sub_ref.at[layer], z_recv.at[1 - side, 0], near_z),
            (oxy_ref.at[layer], z_recv.at[1 - side, 1], near_z),
        ]
        for number, (source, target, device) in enumerate(pairs):
            sem = side * 4 + number
            halos.append(
                pltpu.make_async_remote_copy(
                    src_ref=source,
                    dst_ref=target,
                    send_sem=halo_send_sem.at[sem],
                    recv_sem=halo_recv_sem.at[sem],
                    device_id=device,
                    device_id_type=MESH,
                )
            )
    for copy in halos:
        copy.start()
    for copy in halos:
        copy.wait()

    shape = (4, 32, LANES)
    row_id = iota(shape, 1)
    lane_id = iota(shape, 2)
    inside = [
        (jnp.where(at > 0, 1.0, 0.0), jnp.where(at < count - 1, 1.0, 0.0))
        for at, count in ((gz, DEPTH), (gx, 4), (gy, 4))
    ]
    for field, ref in enumerate(fields):
        center = ref[...]
        layers = slice(field * 4, field * 4 + 4)
        z_low = (z_recv[0, field] * inside[0][0])[None]
        z_high = (z_recv[1, field] * inside[0][1])[None]
        x_low = (x_recv[0, layers, :] * inside[1][0])[:, None, :]
        x_high = (x_recv[1, layers, :] * inside[1][1])[:, None, :]
        y_edges = []
        for side in range(2):
            edge = y_recv[side, field : field + 1, :] * inside[2][side]
            y_edges.append(jnp.broadcast_to(edge, (LANES, LANES)).T.reshape(shape))
        lower = (
            jnp.concatenate([z_low, center[:3]], axis=0),
            jnp.where(row_id == 0, x_low, pltpu.roll(center, 1, 1)),
            jnp.where(lane_id == 0, y_edges[0], pltpu.roll(center, 1, 2)),
        )
        upper = (
            jnp.concatenate([center[1:], z_high], axis=0),
            jnp.where(row_id == 31, x_high, pltpu.roll(center, 31, 1)),
            jnp.where(lane_id == LANES - 1, y_edges[1], pltpu.roll(center, LANES - 1, 2)),
        )
        total = center
        for axis in range(3):
            courant = vel_ref[axis]
            total = total + diffusion * (lower[axis] + upper[axis] - 2.0 * center)
            total = total - jnp.maximum(courant, 0.0) * (center - lower[axis])
            total = total - jnp.minimum(courant, 0.0) * (upper[axis] - center)
        swept_ref[field] = total
        value_ref[field] = total.reshape(LANES, LANES)

    square = (LANES, LANES)
    sub_row = iota(square, 0)
    row_half = sub_row >> 1
    even = (sub_row & 1) == 0

    def gather_sums(step, total):
        rows = pl.ds(pl.multiple_of(step * 8, 8), 8)
        place = pos_ref[step // 4, pl.ds(pl.multiple_of(lax.rem(step, 4) * 8, 8), 8), :]
        first = value_ref[0, rows, :]
        second = value_ref[1, rows, :]
        left, right = [], []
        for row in range(8):
            one = slice(row, row + 1)
            value = jnp.where(even, first[one], second[one])
            coarse = value.astype(jnp.bfloat16).astype(jnp.float32)
            hit = (place[one] >> 7) == row_half
            top = jnp.where(hit, coarse, 0.0).astype(jnp.bfloat16)
            rest = jnp.where(hit, value - coarse, 0.0).astype(jnp.bfloat16)
            left.append(jnp.concatenate([top, rest], axis=0))
            right.append(jnp.where((place[one] & 127) == sub_row, 1.0, 0.0).astype(jnp.bfloat16))
        return total + lax.dot_general(
            jnp.concatenate(left, axis=1),
            jnp.concatenate(right, axis=1),
            (((1,), (1,)), ((), ())),
            preferred_element_type=jnp.float32,
        )

    sums = lax.fori_loop(0, 16, gather_sums, jnp.zeros((2 * LANES, LANES), jnp.float32))
    sums_ref[...] = (sums[:LANES] + sums[LANES:]).reshape(COLS, 8, LANES)

    def exchange(stage, ids, source_of, target):
        copies = []
        for number, device in enumerate(ids):
            copies.append(
                pltpu.make_async_remote_copy(
                    src_ref=source_of(number),
                    dst_ref=target,
                    send_sem=send_sem.at[stage],
                    recv_sem=recv_sem.at[stage],
                    device_id=device,
                    device_id_type=MESH,
                )
            )
        for copy in copies:
            copy.start()

    def arrived(stage, buffer, count):
        part = buffer.at[pl.ds(0, count)]
        pltpu.make_async_copy(part, part, recv_sem.at[stage]).wait()

    def left_here(stage, buffer, count):
        part = buffer.at[pl.ds(0, count)]
        pltpu.make_async_copy(part, part, send_sem.at[stage]).wait()

    exchange(0, col_ids, lambda number: sums_ref.at[col_peers[number]], a_recv.at[column])
    a_recv[column] = sums_ref[column]
    arrived(0, a_recv, COLS - 1)
    part = jnp.sum(a_recv[...], axis=0)
    for block in range(4):
        b_send[block] = part[2 * block : 2 * block + 2, :]
    exchange(1, deep_ids, lambda number: b_send.at[deep_peers[number] // 8], b_recv.at[gz])
    b_recv[gz] = b_send[gz // 8]
    arrived(1, b_recv, DEPTH - 1)
    means = jnp.sum(b_recv[...], axis=0) / CELLS
    mean_sub, mean_oxy = means[0:1, :], means[1:2, :]
    rate = growth_max * mean_sub / (half_substrate + mean_sub) * mean_oxy / (half_oxygen + mean_oxy)
    packed = uptake_gain * rate * bio_ref[0:1, :]
    packed = packed + pltpu.roll(uptake_gain * rate * bio_ref[1:2, :], 32, 1)
    packed = packed + pltpu.roll(rate * bio_ref[2:3, :], 64, 1)

    c_send[0] = packed
    exchange(2, deep_ids, lambda number: c_send.at[0], c_recv.at[gz])
    c_recv[gz] = packed
    arrived(2, c_recv, DEPTH - 1)
    rows = c_recv[...].reshape(DEPTH, LANES)
    wide = (DEPTH, LANES)
    mine = (iota(wide, 1) >> 5) == ((iota(wide, 0) >> 1) & 3)
    for item in range(3):
        turned = rows if item == 0 else pltpu.roll(rows, LANES - 32 * item, 1)
        kept = jnp.where(mine, turned, 0.0)
        for block in range(4):
            at = item * 4 + block
            d_send[0, at : at + 1, :] = jnp.sum(
                kept[8 * block : 8 * block + 8, :], axis=0, keepdims=True
            )
    d_send[0, 12:16, :] = jnp.zeros((4, LANES), jnp.float32)
    exchange(3, col_ids, lambda number: d_send.at[0], d_recv.at[column])
    d_recv[column] = d_send[0]
    arrived(3, d_recv, COLS - 1)
    table_ref[...] = d_recv[...]

    left_here(0, a_recv, COLS - 1)
    left_here(1, b_recv, DEPTH - 1)
    left_here(2, c_recv, DEPTH - 1)
    left_here(3, d_recv, COLS - 1)


def sweep(substrate, oxygen, velocity, pos, bio):
    f32 = jnp.float32
    return pl.pallas_call(
        sweep_kernel,
        out_shape=(
            jax.ShapeDtypeStruct((2,) + substrate.shape, f32),
            jax.ShapeDtypeStruct((COLS, 16, LANES), f32),
        ),
        in_specs=[VMEM_SPEC] * 5,
        out_specs=(VMEM_SPEC, VMEM_SPEC),
        scratch_shapes=[
            pltpu.VMEM((2, 8, LANES), f32),
            pltpu.VMEM((2, 8, LANES), f32),
            pltpu.VMEM((2, 2, LANES), f32),
            pltpu.VMEM((2, 2, LANES), f32),
            pltpu.VMEM((2, 2, 32, LANES), f32),
            pltpu.VMEM((2, LANES, LANES), f32),
            pltpu.VMEM((COLS, 8, LANES), f32),
            pltpu.VMEM((COLS, 8, LANES), f32),
            pltpu.VMEM((4, 2, LANES), f32),
            pltpu.VMEM((DEPTH, 2, LANES), f32),
            pltpu.VMEM((1, 1, LANES), f32),
            pltpu.VMEM((DEPTH, 1, LANES), f32),
            pltpu.VMEM((1, 16, LANES), f32),
            pltpu.VMEM((COLS, 16, LANES), f32),
            pltpu.SemaphoreType.DMA((8,)),
            pltpu.SemaphoreType.DMA((8,)),
            pltpu.SemaphoreType.DMA((4,)),
            pltpu.SemaphoreType.DMA((4,)),
        ],
        compiler_params=pltpu.CompilerParams(
            collective_id=0, has_side_effects=True, vmem_limit_bytes=VMEM_BYTES
        ),
        cost_estimate=pl.CostEstimate(
            flops=1_200_000_000, bytes_accessed=1_000_000, transcendentals=0
        ),
    )(substrate, oxygen, velocity, pos, bio)


def grow_kernel(
    swept_ref,
    pos_ref,
    table_ref,
    list_ref,
    flow_rate_ref,
    growth_ref,
    daughter_ref,
    division_ref,
    pop_ref,
    incoming_ref,
    sub_out_ref,
    oxy_out_ref,
    pop_out_ref,
    state,
    mother_ref,
    rate_rows,
    rate_table,
    rate_of,
    scale_of,
    target_of,
    state_sem,
    table_sem,
):
    depth = lax.axis_index("gz")
    core = depth & 1
    block = (depth >> 1) & 3
    quarter = depth >> 3
    own_column = lax.axis_index("gx") * 4 + lax.axis_index("gy")

    rows = jnp.zeros((COLS, LANES), jnp.float32)
    for part in range(4):
        rows = rows + jnp.where(quarter == part, table_ref[:, 8 + part, :], 0.0)
    rate_rows[...] = rows
    to_scalar = pltpu.make_async_copy(rate_rows, rate_table, table_sem)
    to_scalar.start()

    own = jnp.int32(0)
    for col in range(COLS):
        lowest, highest = list_ref[0, col], list_ref[0, col + 16]
        own = own + jnp.where(highest >= 0, 1, 0) + jnp.where(highest > lowest, 1, 0)

    def fetch_own(slot, carry):
        pltpu.make_async_copy(pop_ref.at[slot], state.at[slot], state_sem.at[0]).start()
        return carry

    lax.fori_loop(0, own, fetch_own, 0)
    to_scalar.wait()

    def lane_of(slot):
        return block * 32 + jnp.where(core == 1, 31 - slot, slot)

    def own_rate(slot, carry):
        rate_of[slot] = rate_table[own_column, lane_of(slot)]
        return carry

    lax.fori_loop(0, own, own_rate, 0)

    def scan_own(col, carry):
        lowest, highest = list_ref[0, col], list_ref[0, col + 16]

        @pl.when(highest >= 0)
        def _():
            scale_of[lowest >> 4] = flow_rate_ref[lowest & 15]
            scale_of[highest >> 4] = flow_rate_ref[highest & 15]

        return carry

    lax.fori_loop(0, COLS, scan_own, 0)

    def scan_arriving(item, count):
        col, rank = item >> 1, item & 1
        lowest, highest = list_ref[0, col + 32], list_ref[0, col + 48]
        key = jnp.where(rank == 0, lowest, highest)
        valid = jnp.where(rank == 0, highest >= 0, highest > lowest)

        @pl.when(valid)
        def _():
            rate_of[count] = rate_table[col, lane_of(key >> 9)]
            scale_of[count] = flow_rate_ref[key & 15]
            target_of[count] = (key >> 4) & 31
            pltpu.make_async_copy(
                incoming_ref.at[col, pl.ds(pl.multiple_of(rank * AGES, AGES), AGES)],
                state.at[count],
                state_sem.at[0],
            ).start()

        return count + jnp.where(valid, 1, 0)

    total = lax.fori_loop(0, 2 * COLS, scan_arriving, own)

    cells = pos_ref[...].reshape(LANES, LANES)
    low, high = cells & 127, cells >> 7

    def find(col, drawn):
        first, second = drawn
        tile = table_ref[col]
        for part in range(4):
            row = col * 4 + part
            first = lookup(tile[part : part + 1, :], low, high, row, first)
            second = lookup(tile[4 + part : 5 + part, :], low, high, row, second)
        return first, second

    zero = jnp.zeros((LANES, LANES), jnp.float32)
    drawn = lax.fori_loop(0, COLS, find, (zero, zero))
    for field, (out, half) in enumerate(
        ((sub_out_ref, half_substrate), (oxy_out_ref, half_oxygen))
    ):
        swept = swept_ref[field]
        out[...] = swept - drawn[field].reshape(swept.shape) * swept / (half + swept)

    def fetched(slot, carry):
        pltpu.make_async_copy(pop_ref.at[0], state.at[slot], state_sem.at[0]).wait()
        return carry

    lax.fori_loop(0, total, fetched, 0)

    groups = (total + GROUP - 1) // GROUP
    for step in range(SUBSTEPS):
        oldest = AGES - 1 - step
        turn = step

        def one_group(group, carry, oldest=oldest, turn=turn):
            base = group * GROUP
            held = state[pl.ds(base, GROUP)]
            moved = jnp.dot(
                held.reshape(GROUP * AGES, SIZES).astype(jnp.bfloat16),
                growth_ref[...],
                preferred_element_type=jnp.float32,
            ).reshape(GROUP, AGES, SIZES)
            for slot in range(GROUP):
                rate = rate_of[base + slot]
                grown = held[slot] + rate * (moved[slot] - held[slot])
                divided = (division_ref[turn] * rate) * grown
                remain = grown - divided
                mother_ref[pl.ds(base + slot, 1), :] = jnp.sum(divided, axis=0, keepdims=True)
                state[base + slot] = remain
                state[base + slot, oldest - 1 : oldest, :] = (
                    remain[oldest - 1 : oldest, :] + remain[oldest : oldest + 1, :]
                )
            return carry

        lax.fori_loop(0, groups, one_group, 0)
        newborn = 2.0 * jnp.dot(
            mother_ref[...].astype(jnp.bfloat16),
            daughter_ref[...],
            preferred_element_type=jnp.float32,
        )
        state[:, oldest, :] = newborn

    top = AGES - SUBSTEPS
    for slot in range(SLOTS):

        @pl.when(slot < own)
        def _():
            kept = state[slot]
            kept = kept - scale_of[slot] * kept
            pop_out_ref[slot, :SUBSTEPS, :] = kept[top:]
            pop_out_ref[slot, SUBSTEPS:, :] = kept[:top]

        @pl.when(slot >= own)
        def _():
            pop_out_ref[slot] = jnp.zeros((AGES, SIZES), jnp.float32)

    def arrive(item, carry):
        slot = target_of[item]
        inflow = scale_of[item] * state[item]
        pop_out_ref[slot, :SUBSTEPS, :] = pop_out_ref[slot, :SUBSTEPS, :] + inflow[top:]
        pop_out_ref[slot, SUBSTEPS:, :] = pop_out_ref[slot, SUBSTEPS:, :] + inflow[:top]
        return carry

    lax.fori_loop(own, total, arrive, 0)


def grow(swept, pos, table, lists, flow_rates, growth, daughter, division, population, incoming):
    f32 = jnp.float32
    field = jax.ShapeDtypeStruct(pos.shape, f32)
    turned = jnp.stack([jnp.roll(division, -step, axis=0) for step in range(SUBSTEPS)])
    return pl.pallas_call(
        grow_kernel,
        out_shape=(field, field, jax.ShapeDtypeStruct(population.shape, f32)),
        in_specs=[VMEM_SPEC] * 3
        + [SMEM_SPEC] * 2
        + [VMEM_SPEC] * 3
        + [ANY_SPEC] * 2,
        out_specs=(VMEM_SPEC,) * 3,
        scratch_shapes=[
            pltpu.VMEM((64, AGES, SIZES), f32),
            pltpu.VMEM((64, SIZES), f32),
            pltpu.VMEM((COLS, LANES), f32),
            pltpu.SMEM((COLS, LANES), f32),
            pltpu.SMEM((64,), f32),
            pltpu.SMEM((64,), f32),
            pltpu.SMEM((64,), jnp.int32),
            pltpu.SemaphoreType.DMA((1,)),
            pltpu.SemaphoreType.DMA,
        ],
        compiler_params=pltpu.CompilerParams(vmem_limit_bytes=VMEM_BYTES),
        cost_estimate=pl.CostEstimate(
            flops=3_000_000_000, bytes_accessed=8_000_000, transcendentals=0
        ),
    )(swept, pos, table, lists, flow_rates, growth, daughter, turned, population, incoming)


def per_device(
    substrate,
    oxygen,
    velocity,
    cell_map,
    owner_slot,
    flow_list,
    flow_rates,
    population,
    growth,
    daughter_kernel,
    division_rate,
    uptake_weight,
):
    pos, bio, lists, payload = prepare(
        owner_slot.reshape(64, LANES), flow_list, cell_map, uptake_weight, population
    )
    incoming = lax.all_to_all(payload, ("gx", "gy"), split_axis=0, concat_axis=0, tiled=True)
    swept, table = sweep(substrate, oxygen, velocity, pos, bio)
    return grow(
        swept,
        pos,
        table,
        lists,
        flow_rates,
        growth,
        daughter_kernel,
        division_rate,
        population,
        incoming,
    )


def solution(mesh):
    return jax.shard_map(
        per_device,
        mesh=mesh,
        in_specs=(
            P("gz", "gx", "gy"),
            P("gz", "gx", "gy"),
            P(None, "gz", "gx", "gy"),
            P("gz", "gx", "gy"),
            P(),
            P(),
            P(),
            P(("gx", "gy", "gz"), None, None),
            P(),
            P(),
            P(),
            P(),
        ),
        out_specs=(P("gz", "gx", "gy"), P("gz", "gx", "gy"), P(("gx", "gy", "gz"), None, None)),
        check_vma=False,
    )
```

time: 808 us -> 121 us (0.15)
  the two profiles are of different devices: /device:TPU:1 before, /device:TPU:35 now
where the time goes in v1:
time: 121 us
  Pallas kernels  105 us (87%)
  local copies, waits for them, and re-layouts  7.72 us (6%)
  starting transfers between devices  7.06 us (6%)
    pallas_call x1, Pallas kernels, sweep(): pl.pallas_call(sweep_kernel, out_shape=(jax.ShapeDtypeStruct((2,) + subst...  61.4 us
    pallas_call x1, Pallas kernels, grow(): pl.pallas_call(grow_kernel, out_shape=(field, field, jax.ShapeDtypeStruct...  34.3 us
    pallas_call x1, Pallas kernels, prepare(): pl.pallas_call(prepare_kernel, out_shape=(jax.ShapeDtypeStruct(cell_map.s...  9.58 us
    unnamed x29, local copies, waits for them, and re-layouts  7.62 us
    all_to_all x1, starting transfers between devices, per_device(): lax.all_to_all(payload, ('gx', 'gy'), split_axis=0, concat_axis=0, tiled=...  7.06 us
  transfers between devices with their start and end apart: 1, of which 0 were waited for; matrix products, arithmetic and copies ran while one was open for 0% of the time, Pallas kernels for 51%

profile of v1, /device:TPU:35, one launch (start us, length us, event | category | flops | bytes accessed | tf_op | source)
XLA Modules:
  0.0 121.1 jit_solution(15251191663025927008)
XLA Ops:
  0.6 0.0 copy-start.1
  0.6 1.6 %copy-done.1 = f32[31,64,256]{2,1,0:T(8,128)S(1)} copy-done((f32[31,64,256]{2,1,0:T(8,128)S(1)}, f32[31,64,256]{2,1,0:T(8,128)}, u32[]{:S(2)}) %copy-start.1) | copy-done | bytes 2031640
  2.2 0.8 copy-done.3
  3.0 0.8 copy-done.4
  3.9 0.8 copy-done.5
  4.6 0.7 copy-done.6
  5.3 9.6 %shard_map.139 = (s32[4,32,128]{2,1,0:T(8,128)S(1)}, f32[8,128]{1,0:T(8,128)S(1)}, s32[1,128]{1,0:T(1,128)S(1)}, f32[16,128,256]{2,1,0:T(8,128)S(1)}) custom-call(s32[64,128]{1,0:T(8,128)S(1)} %bitcast.31, s32[2,8192]{1,0:T(2,128)S(1)} %copy-done.3, s32[4,32,128]{2,1,0:T(8,128)S(1)} %copy-done.4, f32[2,256]{1,0:T(2,128)S(1)} %copy-done.6, ...), custom_call_target="tpu_custom_call" | custom-call | flops 8000000 | bytes 6000000 | tf_op jit(solution)/shard_map/pallas_call | solution.py:171
  14.9 0.0 copy-start
  14.9 1.3 %copy-done = f32[16,128,256]{2,1,0:T(8,128)} copy-done((f32[16,128,256]{2,1,0:T(8,128)}, f32[16,128,256]{2,1,0:T(8,128)S(1)}, u32[]{:S(2)}) %copy-start) | copy-done | bytes 2097176
  16.3 7.1 %all-to-all-start = ((f32[16,128,256]{2,1,0:T(8,128)}), f32[16,128,256]{2,1,0:T(8,128)S(1)}, u32[]{:S(2)}, u32[]{:S(2)}) async-start(f32[16,128,256]{2,1,0:T(8,128)} %copy-done), calls=%async_computation | async-start | bytes 4194304 | tf_op jit(solution)/shard_map/all_to_all | solution.py:670
  23.3 0.0 copy-done.13
  23.5 0.0 copy-done.7
  23.5 0.0 slice-start
  23.5 0.0 slice-start.1
  23.5 0.0 slice-start.3
  23.5 0.0 slice-start.2
  23.5 0.0 slice-start.5
  23.5 0.0 slice-start.4
  23.5 0.0 slice-start.6
  23.6 0.0 copy-start.8
  23.6 0.0 copy-start.9
  23.6 0.0 copy-start.12
  23.6 61.4 %shard_map.140 = (f32[2,4,32,128]{3,2,1,0:T(8,128)S(1)}, f32[16,16,128]{2,1,0:T(8,128)S(1)}) custom-call(f32[4,32,128]{2,1,0:T(8,128)S(1)} %copy-done.10, f32[4,32,128]{2,1,0:T(8,128)S(1)} %copy-done.11, f32[3,4,32,128]{3,2,1,0:T(8,128)S(1)} %copy-done.7, s32[4,32,128]{2,1,0:T(8,128)S(1)} %get-tuple-element.9.pos_ref, f32[8,128]{1,0:T(8,128)S(1)} %get-tuple-element.10.bio_ref), custom_call_target="tpu_custom_call" | custom-call | flops 1200000000 | bytes 1000000 | tf_op jit(solution)/shard_map/pallas_call | solution.py:412
  85.0 0.0 slice-done.1
  85.1 0.0 slice-done.6
  85.2 0.0 all-to-all-done.incoming_ref
  85.2 0.0 copy-done.8
  85.2 0.0 copy-done.9
  85.2 0.0 copy-done.12
  85.2 0.0 copy-start.2
  85.2 1.6 %copy-done.2 = f32[31,64,256]{2,1,0:T(8,128)S(1)} copy-done((f32[31,64,256]{2,1,0:T(8,128)S(1)}, f32[31,64,256]{2,1,0:T(8,128)}, u32[]{:S(2)}) %copy-start.2) | copy-done | bytes 2031640
  86.8 34.3 %shard_map.141 = (f32[4,32,128]{2,1,0:T(8,128)}, f32[4,32,128]{2,1,0:T(8,128)}, f32[31,64,256]{2,1,0:T(8,128)}) custom-call(f32[2,4,32,128]{3,2,1,0:T(8,128)S(1)} %get-tuple-element.11.swept_ref, s32[4,32,128]{2,1,0:T(8,128)S(1)} %get-tuple-element.9.pos_ref, f32[16,16,128]{2,1,0:T(8,128)S(1)} %get-tuple-element.12.table_ref, ...), custom_call_target="tpu_custom_call" | custom-call | flops 3000000000 | bytes 8000000 | tf_op jit(solution)/shard_map/pallas_call | solution.py:627
  (30 shorter events, 0.2 us)
Async XLA Ops:
  0.6 1.6 %copy-start.1 = (f32[31,64,256]{2,1,0:T(8,128)S(1)}, f32[31,64,256]{2,1,0:T(8,128)}, u32[]{:S(2)}) copy-start(f32[31,64,256]{2,1,0:T(8,128)} %pop_ref.3) | copy-start | bytes 6094852
  2.2 0.8 copy-start.3
  3.0 0.8 copy-start.4
  3.9 0.8 copy-start.5
  4.6 0.7 copy-start.6
  14.9 1.3 %copy-start = (f32[16,128,256]{2,1,0:T(8,128)}, f32[16,128,256]{2,1,0:T(8,128)S(1)}, u32[]{:S(2)}) copy-start(f32[16,128,256]{2,1,0:T(8,128)S(1)} %get-tuple-element.14) | copy-start | bytes 6291460
  16.3 7.1 %copy-start.13 = (f32[64,256]{1,0:T(8,128)S(1)}, f32[64,256]{1,0:T(8,128)}, u32[]{:S(2)}) copy-start(f32[64,256]{1,0:T(8,128)} %param.22) | copy-start | bytes 196612
  16.3 7.2 %copy-start.7 = (f32[3,4,32,128]{3,2,1,0:T(8,128)S(1)}, f32[3,4,32,128]{3,2,1,0:T(8,128)}, u32[]{:S(2)}) copy-start(f32[3,4,32,128]{3,2,1,0:T(8,128)} %vel_ref.1) | copy-start | bytes 589828
  16.3 7.2 %copy-start.10 = (f32[4,32,128]{2,1,0:T(8,128)S(1)}, f32[4,32,128]{2,1,0:T(8,128)}, u32[]{:S(2)}) copy-start(f32[4,32,128]{2,1,0:T(8,128)} %sub_ref.1) | copy-start | bytes 196612
  16.3 7.2 %copy-start.11 = (f32[4,32,128]{2,1,0:T(8,128)S(1)}, f32[4,32,128]{2,1,0:T(8,128)}, u32[]{:S(2)}) copy-start(f32[4,32,128]{2,1,0:T(8,128)} %oxy_ref.1) | copy-start | bytes 196612
  16.3 68.9 %all-to-all-start = ((f32[16,128,256]{2,1,0:T(8,128)}), f32[16,128,256]{2,1,0:T(8,128)S(1)}, u32[]{:S(2)}, u32[]{:S(2)}) async-start(f32[16,128,256]{2,1,0:T(8,128)} %copy-done), calls=%async_computation | async-start | bytes 4194304 | tf_op jit(solution)/shard_map/all_to_all | solution.py:670
  23.5 61.5 %slice-start = ((f32[64,256]{1,0:T(8,128)}), f32[1,256]{1,0:T(1,128)S(1)}, s32[]{:S(2)}) async-start(f32[64,256]{1,0:T(8,128)} %param.22), calls=%async_computation.1 | async-start | bytes 2048 | tf_op jit(solution)/shard_map/jit(_roll_static)/slice | solution.py:626
  23.5 61.5 %slice-start.1 = ((f32[64,256]{1,0:T(8,128)}), f32[2,256]{1,0:T(2,128)S(1)}, s32[]{:S(2)}) async-start(f32[64,256]{1,0:T(8,128)} %param.22), calls=%async_computation.2 | async-start | bytes 4096 | tf_op jit(solution)/shard_map/jit(_roll_static)/slice | solution.py:626
  23.5 61.5 %slice-start.3 = ((f32[64,256]{1,0:T(8,128)}), f32[3,256]{1,0:T(4,128)S(1)}, s32[]{:S(2)}) async-start(f32[64,256]{1,0:T(8,128)} %param.22), calls=%async_computation.4 | async-start | bytes 8192 | tf_op jit(solution)/shard_map/jit(_roll_static)/slice | solution.py:626
  23.5 61.5 %slice-start.2 = ((f32[64,256]{1,0:T(8,128)}), f32[4,256]{1,0:T(4,128)S(1)}, s32[]{:S(2)}) async-start(f32[64,256]{1,0:T(8,128)} %param.22), calls=%async_computation.3 | async-start | bytes 8192 | tf_op jit(solution)/shard_map/jit(_roll_static)/slice | solution.py:626
  23.5 61.6 %slice-start.5 = ((f32[64,256]{1,0:T(8,128)}), f32[5,256]{1,0:T(8,128)S(1)}, s32[]{:S(2)}) async-start(f32[64,256]{1,0:T(8,128)} %param.22), calls=%async_computation.6 | async-start | bytes 16384 | tf_op jit(solution)/shard_map/jit(_roll_static)/slice | solution.py:626
  23.5 61.6 %slice-start.4 = ((f32[64,256]{1,0:T(8,128)}), f32[6,256]{1,0:T(8,128)S(1)}, s32[]{:S(2)}) async-start(f32[64,256]{1,0:T(8,128)} %param.22), calls=%async_computation.5 | async-start | bytes 16384 | tf_op jit(solution)/shard_map/jit(_roll_static)/slice | solution.py:626
  23.5 61.6 %slice-start.6 = ((f32[64,256]{1,0:T(8,128)}), f32[7,256]{1,0:T(8,128)S(1)}, s32[]{:S(2)}) async-start(f32[64,256]{1,0:T(8,128)} %param.22), calls=%async_computation.7 | async-start | bytes 16384 | tf_op jit(solution)/shard_map/jit(_roll_static)/slice | solution.py:626
  23.6 61.6 %copy-start.8 = (bf16[256,256]{1,0:T(8,128)(2,1)S(1)}, bf16[256,256]{1,0:T(8,128)(2,1)}, u32[]{:S(2)}) copy-start(bf16[256,256]{1,0:T(8,128)(2,1)} %growth_ref.1) | copy-start | bytes 393220
  23.6 61.6 %copy-start.9 = (bf16[256,256]{1,0:T(8,128)(2,1)S(1)}, bf16[256,256]{1,0:T(8,128)(2,1)}, u32[]{:S(2)}) copy-start(bf16[256,256]{1,0:T(8,128)(2,1)} %daughter_ref.1) | copy-start | bytes 393220
  23.6 61.6 %copy-start.12 = (f32[16]{0:T(128)S(1)}, f32[16]{0:T(128)}, u32[]{:S(2)}) copy-start(f32[16]{0:T(128)} %flow_rate_ref.1) | copy-start | bytes 196
  85.2 1.6 %copy-start.2 = (f32[31,64,256]{2,1,0:T(8,128)S(1)}, f32[31,64,256]{2,1,0:T(8,128)}, u32[]{:S(2)}) copy-start(f32[31,64,256]{2,1,0:T(8,128)} %pop_ref.3) | copy-start | bytes 6094852

commit v2 on v1

v2 whole, which is shorter than its diff:
```python
import functools

import jax
import jax.numpy as jnp
from jax import lax
from jax.experimental import pallas as pl
from jax.experimental.pallas import tpu as pltpu
from jax.sharding import PartitionSpec as P

SUBSTEPS = 8
CELLS = 1024
SLOTS = 31
AGES = 64
SIZES = 256
COLS = 16
DEPTH = 32
LANES = 128
GROUP = 8
NONE_KEY = 65536.0

diffusion = 0.05
growth_max = 0.8
half_substrate = 0.3
half_oxygen = 0.1
uptake_gain = 3.0

FLOW_PARTS = (
    ((1, 0), (3, 0), (0, 1), (0, 3)),
    ((2, 0), (0, 2), (1, 1), (3, 3), (1, 3), (3, 1)),
    ((1, 2), (2, 1), (2, 3), (3, 2), (2, 2)),
)

MESH = pl.DeviceIdType.MESH
VMEM_SPEC = pl.BlockSpec(memory_space=pltpu.VMEM)
SMEM_SPEC = pl.BlockSpec(memory_space=pltpu.SMEM)
HBM_SPEC = pl.BlockSpec(memory_space=pltpu.HBM)
VMEM_BYTES = 48 * 1024 * 1024


def iota(shape, dim):
    return lax.broadcasted_iota(jnp.int32, shape, dim)


def device_of(slot):
    return (slot * 33826) >> 20


def lookup(table_row, index, high, row_id, total):
    row = jnp.broadcast_to(table_row, index.shape)
    found = jnp.take_along_axis(row, index, axis=1, mode="promise_in_bounds")
    return jnp.where(high == row_id, found, total)


def prepare_kernel(
    owner_hbm,
    flow_hbm,
    pop_ref,
    list_ref,
    payload_ref,
    owner_ref,
    flow_ref,
    target_ref,
    index_ref,
    row_ref,
    list_smem,
    load_sem,
    list_sem,
    pay_sem,
):
    column = lax.axis_index("gx") * 4 + lax.axis_index("gy")
    me = column * DEPTH + lax.axis_index("gz")
    loads = [
        pltpu.make_async_copy(owner_hbm, owner_ref, load_sem.at[0]),
        pltpu.make_async_copy(flow_hbm, flow_ref, load_sem.at[1]),
    ]
    for load in loads:
        load.start()
    for load in loads:
        load.wait()
    for row in range(64):
        lanes = slice(row * LANES, (row + 1) * LANES)
        target_ref[row : row + 1, :] = flow_ref[0:1, lanes]
        index_ref[row : row + 1, :] = flow_ref[1:2, lanes]

    owner = owner_ref[...]
    targets = target_ref[...]
    low, high = targets & 127, targets >> 7
    target_slot = jnp.zeros_like(owner)
    for row in range(64):
        target_slot = lookup(owner_ref[row : row + 1, :], low, high, row, target_slot)
    rate_index = index_ref[...]
    source_dev = device_of(owner)
    source_local = owner - source_dev * SLOTS
    target_dev = device_of(target_slot)
    target_local = target_slot - target_dev * SLOTS
    send_key = (source_local * 16 + rate_index).astype(jnp.float32)
    recv_key = (source_local * 512 + target_local * 16 + rate_index).astype(jnp.float32)
    send_col = jnp.where(source_dev == me, target_dev >> 5, -1)
    recv_col = jnp.where(target_dev == me, source_dev >> 5, -1)
    for col in range(COLS):
        for kind, (key, cols) in enumerate(((send_key, send_col), (recv_key, recv_col))):
            hit = cols == col
            low_row = jnp.min(jnp.where(hit, key, NONE_KEY), axis=0, keepdims=True)
            high_row = jnp.max(jnp.where(hit, key, -1.0), axis=0, keepdims=True)
            at = kind * 32 + col
            row_ref[at : at + 1, :] = low_row
            row_ref[at + 16 : at + 17, :] = high_row
    square = (64, LANES)
    rows = row_ref[...]
    is_low = (iota((64, 1), 0) & 16) == 0
    reduced = jnp.where(
        is_low, jnp.min(rows, axis=1, keepdims=True), jnp.max(rows, axis=1, keepdims=True)
    )
    diagonal = jnp.where(iota(square, 0) == iota(square, 1), reduced, 0.0)
    list_ref[...] = jnp.sum(diagonal, axis=0, keepdims=True).astype(jnp.int32)
    to_scalar = pltpu.make_async_copy(list_ref, list_smem, list_sem)
    to_scalar.start()
    to_scalar.wait()
    for col in range(COLS):
        lowest, highest = list_smem[0, col], list_smem[0, col + 16]
        first = jnp.where(highest >= 0, lowest >> 4, 0)
        second = jnp.where(highest >= 0, highest >> 4, 0)
        for rank, slot in enumerate((first, second)):
            pltpu.make_async_copy(
                pop_ref.at[slot],
                payload_ref.at[col, pl.ds(rank * AGES, AGES)],
                pay_sem.at[col * 2 + rank],
            ).start()
    for item in range(2 * COLS):
        pltpu.make_async_copy(
            pop_ref.at[0],
            payload_ref.at[item // 2, pl.ds((item % 2) * AGES, AGES)],
            pay_sem.at[item],
        ).wait()


def prepare(owner, flow, population):
    return pl.pallas_call(
        prepare_kernel,
        out_shape=(
            jax.ShapeDtypeStruct((1, LANES), jnp.int32),
            jax.ShapeDtypeStruct((COLS, 2 * AGES, SIZES), jnp.float32),
        ),
        in_specs=[HBM_SPEC, HBM_SPEC, HBM_SPEC],
        out_specs=(VMEM_SPEC, HBM_SPEC),
        scratch_shapes=[
            pltpu.VMEM((64, LANES), jnp.int32),
            pltpu.VMEM(flow.shape, jnp.int32),
            pltpu.VMEM((64, LANES), jnp.int32),
            pltpu.VMEM((64, LANES), jnp.int32),
            pltpu.VMEM((64, LANES), jnp.float32),
            pltpu.SMEM((1, LANES), jnp.int32),
            pltpu.SemaphoreType.DMA((2,)),
            pltpu.SemaphoreType.DMA,
            pltpu.SemaphoreType.DMA((2 * COLS,)),
        ],
        compiler_params=pltpu.CompilerParams(vmem_limit_bytes=16 * 1024 * 1024),
        cost_estimate=pl.CostEstimate(flops=8_000_000, bytes_accessed=6_000_000, transcendentals=0),
    )(owner, flow, population)


def grow_rounds(state, rate_of, mother_ref, turned_ref, growth_ref, daughter_ref, groups):
    for step in range(SUBSTEPS):
        oldest = AGES - 1 - step

        def one_group(group, carry, oldest=oldest, step=step):
            base = group * GROUP
            held = state[pl.ds(base, GROUP)]
            moved = jnp.dot(
                held.reshape(GROUP * AGES, SIZES).astype(jnp.bfloat16),
                growth_ref[...],
                preferred_element_type=jnp.float32,
            ).reshape(GROUP, AGES, SIZES)
            for slot in range(GROUP):
                rate = rate_of(base + slot)
                grown = held[slot] + rate * (moved[slot] - held[slot])
                divided = (turned_ref[step] * rate) * grown
                remain = grown - divided
                mother_ref[pl.ds(base + slot, 1), :] = jnp.sum(divided, axis=0, keepdims=True)
                state[base + slot] = remain
                state[base + slot, oldest - 1 : oldest, :] = (
                    remain[oldest - 1 : oldest, :] + remain[oldest : oldest + 1, :]
                )
            return carry

        lax.fori_loop(0, groups, one_group, 0)
        newborn = 2.0 * jnp.dot(
            mother_ref[...].astype(jnp.bfloat16),
            daughter_ref[...],
            preferred_element_type=jnp.float32,
        )
        state[:, oldest, :] = newborn


def sweep_kernel(
    sub_ref,
    oxy_ref,
    vel_ref,
    map_ref,
    owner_ref,
    weight_ref,
    growth_ref,
    daughter_ref,
    division_ref,
    pop_ref,
    payload_ref,
    swept_ref,
    pos_ref,
    table_ref,
    turned_ref,
    state_ref,
    incoming_ref,
    x_send,
    x_recv,
    y_send,
    y_recv,
    z_recv,
    place_ref,
    ages_ref,
    mother_ref,
    value_ref,
    sums_ref,
    a_recv,
    pair_send,
    pair_recv,
    deep_send,
    deep_recv,
    bio_send,
    bio_recv,
    d_send,
    d_recv,
    rate_row,
    rate_smem,
    local_sem,
    halo_send_sem,
    halo_recv_sem,
    flow_send_sem,
    flow_recv_sem,
    send_sem,
    recv_sem,
):
    gx, gy, gz = lax.axis_index("gx"), lax.axis_index("gy"), lax.axis_index("gz")
    column = gx * 4 + gy
    chip, core = gz // 2, lax.rem(gz, 2)
    col_peers = [lax.rem(column + step, COLS) for step in range(1, COLS)]
    col_ids = [(peer // 4, lax.rem(peer, 4), gz) for peer in col_peers]
    deep_ids = [(gx, gy, lax.rem(gz + step, DEPTH)) for step in range(1, DEPTH)]
    same_core_ids = [(gx, gy, lax.rem(gz + step, DEPTH)) for step in range(2, DEPTH, 2)]
    sibling = (gx, gy, gz + 1 - 2 * core)

    barrier = pltpu.get_barrier_semaphore()
    for peer in col_ids + deep_ids:
        pl.semaphore_signal(barrier, inc=1, device_id=peer, device_id_type=MESH)
    load = pltpu.make_async_copy(pop_ref, state_ref.at[pl.ds(0, SLOTS)], local_sem.at[0])
    load.start()
    stay = pltpu.make_async_copy(
        payload_ref.at[column], incoming_ref.at[column], local_sem.at[1]
    )
    stay.start()

    def send(stage, ids, source_of, target):
        for number, device in enumerate(ids):
            pltpu.make_async_remote_copy(
                src_ref=source_of(number),
                dst_ref=target,
                send_sem=send_sem.at[stage],
                recv_sem=recv_sem.at[stage],
                device_id=device,
                device_id_type=MESH,
            ).start()

    def arrived(stage, buffer, count):
        part = buffer.at[pl.ds(0, count)]
        pltpu.make_async_copy(part, part, recv_sem.at[stage]).wait()

    def left_here(stage, buffer, count):
        part = buffer.at[pl.ds(0, count)]
        pltpu.make_async_copy(part, part, send_sem.at[stage]).wait()

    flows = []

    def send_flows(part):
        for step_x, step_y in FLOW_PARTS[part]:
            near_x, near_y = lax.rem(gx + step_x, 4), lax.rem(gy + step_y, 4)
            number = len(flows)
            copy = pltpu.make_async_remote_copy(
                src_ref=payload_ref.at[near_x * 4 + near_y],
                dst_ref=incoming_ref.at[column],
                send_sem=flow_send_sem.at[number],
                recv_sem=flow_recv_sem.at[number],
                device_id=(near_x, near_y, gz),
                device_id_type=MESH,
            )
            copy.start()
            flows.append(copy)

    fields = (sub_ref, oxy_ref)
    for field, ref in enumerate(fields):
        layers = slice(field * 4, field * 4 + 4)
        x_send[0, layers, :] = ref[:, 0, :]
        x_send[1, layers, :] = ref[:, 31, :]
        turned = ref[...].reshape(LANES, LANES).T
        y_send[0, field : field + 1, :] = turned[0:1, :]
        y_send[1, field : field + 1, :] = turned[LANES - 1 : LANES, :]

    owner = owner_ref[...]
    owner_dev = device_of(owner)
    owner_local = owner - owner_dev * SLOTS
    place_ref[...] = (owner_dev >> 1) * 32 + jnp.where(
        (owner_dev & 1) == 1, 31 - owner_local, owner_local
    )
    cells = map_ref[...].reshape(LANES, LANES)
    low, high = cells & 127, cells >> 7

    def find(step, total):
        for part in range(8):
            row = step * 8 + part
            total = lookup(place_ref[pl.ds(row, 1), :], low, high, row, total)
        return total

    place = lax.fori_loop(0, 8, find, jnp.zeros_like(cells))
    pos_ref[...] = place.reshape(pos_ref.shape)

    division = division_ref[...]
    turned_ref[0] = division
    for step in range(1, SUBSTEPS):
        turned_ref[step] = pltpu.roll(division, AGES - step, 0)

    load.wait()
    state_ref[SLOTS] = jnp.zeros((AGES, SIZES), jnp.float32)
    for slot in range(SLOTS + 1):
        ages_ref[slot : slot + 1, :] = jnp.sum(state_ref[slot], axis=0, keepdims=True)
    summed = ages_ref[...]
    owned = jnp.where(owner_dev == column * DEPTH + gz, 1.0, 0.0)
    held = jnp.sum(jnp.sum(owned, axis=0, keepdims=True), axis=1, keepdims=True)
    block = lax.rem(chip, 4)
    wide = (DEPTH, LANES)
    lane = iota(wide, 1)
    local = lane & 31
    slot_of_lane = jnp.where(core == 1, 31 - local, local)
    here = ((lane >> 5) == block) & (slot_of_lane == iota(wide, 0))
    here = here & (slot_of_lane.astype(jnp.float32) < held)
    masses = []
    for field in range(2):
        weighted = summed * weight_ref[field : field + 1, :]
        mass = jnp.sum(weighted, axis=1, keepdims=True) / (AGES * SIZES)
        masses.append(jnp.sum(jnp.where(here, mass, 0.0), axis=0, keepdims=True))
    packed = masses[0] + pltpu.roll(masses[1], 32, 1)
    bio_send[0] = packed
    bio_recv[gz] = packed

    pl.semaphore_wait(barrier, len(col_ids) + len(deep_ids))

    halos = []
    for side in range(2):
        step = 3 if side == 0 else 1
        near_x = (lax.rem(gx + step, 4), gy, gz)
        near_y = (gx, lax.rem(gy + step, 4), gz)
        near_z = (gx, gy, lax.rem(gz + (DEPTH - 1 if side == 0 else 1), DEPTH))
        layer = 0 if side == 0 else 3
        pairs = [
            (x_send.at[side], x_recv.at[1 - side], near_x),
            (y_send.at[side], y_recv.at[1 - side], near_y),
            (sub_ref.at[layer], z_recv.at[1 - side, 0], near_z),
            (oxy_ref.at[layer], z_recv.at[1 - side, 1], near_z),
        ]
        for number, (source, target, device) in enumerate(pairs):
            sem = side * 4 + number
            halos.append(
                pltpu.make_async_remote_copy(
                    src_ref=source,
                    dst_ref=target,
                    send_sem=halo_send_sem.at[sem],
                    recv_sem=halo_recv_sem.at[sem],
                    device_id=device,
                    device_id_type=MESH,
                )
            )
    for copy in halos:
        copy.start()
    send(0, deep_ids, lambda number: bio_send.at[0], bio_recv.at[gz])
    for copy in halos:
        copy.wait()
    send_flows(0)

    shape = (4, 32, LANES)
    row_id = iota(shape, 1)
    lane_id = iota(shape, 2)
    inside = [
        (jnp.where(at > 0, 1.0, 0.0), jnp.where(at < count - 1, 1.0, 0.0))
        for at, count in ((gz, DEPTH), (gx, 4), (gy, 4))
    ]
    for field, ref in enumerate(fields):
        center = ref[...]
        layers = slice(field * 4, field * 4 + 4)
        z_low = (z_recv[0, field] * inside[0][0])[None]
        z_high = (z_recv[1, field] * inside[0][1])[None]
        x_low = (x_recv[0, layers, :] * inside[1][0])[:, None, :]
        x_high = (x_recv[1, layers, :] * inside[1][1])[:, None, :]
        y_edges = []
        for side in range(2):
            edge = y_recv[side, field : field + 1, :] * inside[2][side]
            y_edges.append(jnp.broadcast_to(edge, (LANES, LANES)).T.reshape(shape))
        lower = (
            jnp.concatenate([z_low, center[:3]], axis=0),
            jnp.where(row_id == 0, x_low, pltpu.roll(center, 1, 1)),
            jnp.where(lane_id == 0, y_edges[0], pltpu.roll(center, 1, 2)),
        )
        upper = (
            jnp.concatenate([center[1:], z_high], axis=0),
            jnp.where(row_id == 31, x_high, pltpu.roll(center, 31, 1)),
            jnp.where(lane_id == LANES - 1, y_edges[1], pltpu.roll(center, LANES - 1, 2)),
        )
        total = center
        for axis in range(3):
            courant = vel_ref[axis]
            total = total + diffusion * (lower[axis] + upper[axis] - 2.0 * center)
            total = total - jnp.maximum(courant, 0.0) * (center - lower[axis])
            total = total - jnp.minimum(courant, 0.0) * (upper[axis] - center)
        swept_ref[field] = total
        value_ref[field] = total.reshape(LANES, LANES)

    fine_row = iota((2 * LANES, LANES), 0)
    sub_row = iota((64, LANES), 0)
    row_half = sub_row >> 1
    even = (sub_row & 1) == 0

    def gather_sums(step, total):
        rows = pl.ds(pl.multiple_of(step * 8, 8), 8)
        place = pos_ref[step // 4, pl.ds(pl.multiple_of(lax.rem(step, 4) * 8, 8), 8), :]
        first = value_ref[0, rows, :]
        second = value_ref[1, rows, :]
        left, right = [], []
        for row in range(8):
            one = slice(row, row + 1)
            value = jnp.where(even, first[one], second[one])
            coarse = value.astype(jnp.bfloat16).astype(jnp.float32)
            hit = (place[one] >> 8) == row_half
            top = jnp.where(hit, coarse, 0.0).astype(jnp.bfloat16)
            rest = jnp.where(hit, value - coarse, 0.0).astype(jnp.bfloat16)
            left.append(jnp.concatenate([top, rest], axis=0))
            right.append(jnp.where((place[one] & 255) == fine_row, 1.0, 0.0).astype(jnp.bfloat16))
        return total + lax.dot_general(
            jnp.concatenate(left, axis=1),
            jnp.concatenate(right, axis=1),
            (((1,), (1,)), ((), ())),
            preferred_element_type=jnp.float32,
        )

    sums = lax.fori_loop(0, 16, gather_sums, jnp.zeros((LANES, 2 * LANES), jnp.float32))
    sums_ref[...] = (sums[:64] + sums[64:]).reshape(COLS, 4, 2 * LANES)

    send(1, col_ids, lambda number: sums_ref.at[col_peers[number]], a_recv.at[column])
    a_recv[column] = sums_ref[column]
    arrived(1, a_recv, COLS - 1)
    send_flows(1)
    part = jnp.sum(a_recv[...], axis=0)
    split = []
    for field in range(2):
        split.append(
            jnp.concatenate(
                [
                    part[2 * (row // 2) + field : 2 * (row // 2) + field + 1][
                        :, (row % 2) * LANES : (row % 2 + 1) * LANES
                    ]
                    for row in range(4)
                ],
                axis=0,
            )
        )

    first_core = core == 0
    pair_send[0] = jnp.where(first_core, split[1], split[0])
    send(2, [sibling], lambda number: pair_send.at[0], pair_recv.at[0])
    arrived(2, pair_recv, 1)
    chip_sum = jnp.where(first_core, split[0], split[1]) + pair_recv[0]
    deep_send[0] = chip_sum
    send(3, same_core_ids, lambda number: deep_send.at[0], deep_recv.at[chip])
    deep_recv[chip] = chip_sum
    arrived(3, deep_recv, 15)
    added = jnp.sum(deep_recv[...], axis=0)
    pair_send[1] = added
    send(4, [sibling], lambda number: pair_send.at[1], pair_recv.at[1])
    arrived(4, pair_recv, 1)
    other = pair_recv[1]
    mean_sub = jnp.where(first_core, added, other) / CELLS
    mean_oxy = jnp.where(first_core, other, added) / CELLS
    rate = growth_max * mean_sub / (half_substrate + mean_sub) * mean_oxy / (half_oxygen + mean_oxy)

    own_row = jnp.zeros((1, LANES), jnp.float32)
    for row in range(4):
        own_row = own_row + jnp.where(gz // 8 == row, rate[row : row + 1, :], 0.0)
    rate_row[...] = own_row
    to_scalar = pltpu.make_async_copy(rate_row, rate_smem, local_sem.at[2])
    to_scalar.start()

    arrived(0, bio_recv, DEPTH - 1)
    rows = bio_recv[...].reshape(DEPTH, LANES)
    mine = (lane >> 5) == ((iota(wide, 0) >> 1) & 3)
    for field in range(2):
        turned = rows if field == 0 else pltpu.roll(rows, LANES - 32, 1)
        kept = jnp.where(mine, turned, 0.0)
        for row in range(4):
            mass = jnp.sum(kept[8 * row : 8 * row + 8, :], axis=0, keepdims=True)
            at = field * 4 + row
            d_send[0, at : at + 1, :] = uptake_gain * rate[row : row + 1, :] * mass
    d_send[0, 8:12, :] = rate
    d_send[0, 12:16, :] = jnp.zeros((4, LANES), jnp.float32)
    send(5, col_ids, lambda number: d_send.at[0], d_recv.at[column])
    d_recv[column] = d_send[0]
    send_flows(2)

    to_scalar.wait()

    def rate_of(slot):
        return rate_smem[0, block * 32 + jnp.where(core == 1, 31 - slot, slot)]

    grow_rounds(state_ref, rate_of, mother_ref, turned_ref, growth_ref, daughter_ref, 4)

    arrived(5, d_recv, COLS - 1)
    table_ref[...] = d_recv[...]
    left_here(0, bio_recv, DEPTH - 1)
    left_here(1, a_recv, COLS - 1)
    left_here(2, pair_recv, 1)
    left_here(3, deep_recv, 15)
    left_here(4, pair_recv, 1)
    left_here(5, d_recv, COLS - 1)
    stay.wait()
    for copy in flows:
        copy.wait()


def sweep(sub, oxy, velocity, cell_map, owner, weight, growth, daughter, division, pop, payload):
    f32 = jnp.float32
    shape = jax.ShapeDtypeStruct
    return pl.pallas_call(
        sweep_kernel,
        out_shape=(
            shape((2,) + sub.shape, f32),
            shape(sub.shape, jnp.int32),
            shape((COLS, 16, LANES), f32),
            shape((SUBSTEPS, AGES, SIZES), f32),
            shape((SLOTS + 1, AGES, SIZES), f32),
            shape(payload.shape, f32),
        ),
        in_specs=[VMEM_SPEC] * 9 + [HBM_SPEC] * 2,
        out_specs=(VMEM_SPEC,) * 5 + (HBM_SPEC,),
        scratch_shapes=[
            pltpu.VMEM((2, 8, LANES), f32),
            pltpu.VMEM((2, 8, LANES), f32),
            pltpu.VMEM((2, 2, LANES), f32),
            pltpu.VMEM((2, 2, LANES), f32),
            pltpu.VMEM((2, 2, 32, LANES), f32),
            pltpu.VMEM((64, LANES), jnp.int32),
            pltpu.VMEM((SLOTS + 1, SIZES), f32),
            pltpu.VMEM((SLOTS + 1, SIZES), f32),
            pltpu.VMEM((2, LANES, LANES), f32),
            pltpu.VMEM((COLS, 4, 2 * LANES), f32),
            pltpu.VMEM((COLS, 4, 2 * LANES), f32),
            pltpu.VMEM((2, 4, LANES), f32),
            pltpu.VMEM((2, 4, LANES), f32),
            pltpu.VMEM((1, 4, LANES), f32),
            pltpu.VMEM((16, 4, LANES), f32),
            pltpu.VMEM((1, 1, LANES), f32),
            pltpu.VMEM((DEPTH, 1, LANES), f32),
            pltpu.VMEM((1, 16, LANES), f32),
            pltpu.VMEM((COLS, 16, LANES), f32),
            pltpu.VMEM((1, LANES), f32),
            pltpu.SMEM((1, LANES), f32),
            pltpu.SemaphoreType.DMA((3,)),
            pltpu.SemaphoreType.DMA((8,)),
            pltpu.SemaphoreType.DMA((8,)),
            pltpu.SemaphoreType.DMA((COLS - 1,)),
            pltpu.SemaphoreType.DMA((COLS - 1,)),
            pltpu.SemaphoreType.DMA((6,)),
            pltpu.SemaphoreType.DMA((6,)),
        ],
        compiler_params=pltpu.CompilerParams(
            collective_id=0, has_side_effects=True, vmem_limit_bytes=VMEM_BYTES
        ),
        cost_estimate=pl.CostEstimate(
            flops=3_200_000_000, bytes_accessed=8_000_000, transcendentals=0
        ),
    )(sub, oxy, velocity, cell_map, owner, weight, growth, daughter, division, pop, payload)


def finish_kernel(
    swept_ref,
    pos_ref,
    table_ref,
    list_ref,
    flow_rate_ref,
    growth_ref,
    daughter_ref,
    turned_ref,
    own_ref,
    incoming_ref,
    sub_out_ref,
    oxy_out_ref,
    pop_out_ref,
    state,
    mother_ref,
    rate_rows,
    rate_table,
    rate_list,
    scale_of,
    own_scale,
    target_of,
    state_sem,
    table_sem,
):
    depth = lax.axis_index("gz")
    core = depth & 1
    block = (depth >> 1) & 3
    quarter = depth >> 3

    rows = jnp.zeros((COLS, LANES), jnp.float32)
    for part in range(4):
        rows = rows + jnp.where(quarter == part, table_ref[:, 8 + part, :], 0.0)
    rate_rows[...] = rows
    to_scalar = pltpu.make_async_copy(rate_rows, rate_table, table_sem)
    to_scalar.start()
    to_scalar.wait()

    def scan_own(col, count):
        lowest, highest = list_ref[0, col], list_ref[0, col + 16]

        @pl.when(highest >= 0)
        def _():
            own_scale[lowest >> 4] = flow_rate_ref[lowest & 15]
            own_scale[highest >> 4] = flow_rate_ref[highest & 15]

        return count + jnp.where(highest >= 0, 1, 0) + jnp.where(highest > lowest, 1, 0)

    own = lax.fori_loop(0, COLS, scan_own, jnp.int32(0))

    def scan_arriving(item, count):
        col, rank = item >> 1, item & 1
        lowest, highest = list_ref[0, col + 32], list_ref[0, col + 48]
        key = jnp.where(rank == 0, lowest, highest)
        valid = jnp.where(rank == 0, highest >= 0, highest > lowest)

        @pl.when(valid)
        def _():
            slot = key >> 9
            lane = block * 32 + jnp.where(core == 1, 31 - slot, slot)
            rate_list[count] = rate_table[col, lane]
            scale_of[count] = flow_rate_ref[key & 15]
            target_of[count] = (key >> 4) & 31
            pltpu.make_async_copy(
                incoming_ref.at[col, pl.ds(pl.multiple_of(rank * AGES, AGES), AGES)],
                state.at[count],
                state_sem.at[0],
            ).start()

        return count + jnp.where(valid, 1, 0)

    total = lax.fori_loop(0, 2 * COLS, scan_arriving, jnp.int32(0))

    cells = pos_ref[...].reshape(LANES, LANES)
    low, high = cells & 127, cells >> 7

    def find(col, drawn):
        first, second = drawn
        tile = table_ref[col]
        for part in range(4):
            row = col * 4 + part
            first = lookup(tile[part : part + 1, :], low, high, row, first)
            second = lookup(tile[4 + part : 5 + part, :], low, high, row, second)
        return first, second

    zero = jnp.zeros((LANES, LANES), jnp.float32)
    drawn = lax.fori_loop(0, COLS, find, (zero, zero))
    for field, (out, half) in enumerate(
        ((sub_out_ref, half_substrate), (oxy_out_ref, half_oxygen))
    ):
        swept = swept_ref[field]
        out[...] = swept - drawn[field].reshape(swept.shape) * swept / (half + swept)

    def fetched(slot, carry):
        pltpu.make_async_copy(
            incoming_ref.at[0, pl.ds(0, AGES)], state.at[slot], state_sem.at[0]
        ).wait()
        return carry

    lax.fori_loop(0, total, fetched, 0)
    grow_rounds(
        state,
        lambda slot: rate_list[slot],
        mother_ref,
        turned_ref,
        growth_ref,
        daughter_ref,
        (total + GROUP - 1) // GROUP,
    )

    top = AGES - SUBSTEPS
    for slot in range(SLOTS):

        @pl.when(slot < own)
        def _():
            kept = own_ref[slot]
            kept = kept - own_scale[slot] * kept
            pop_out_ref[slot, :SUBSTEPS, :] = kept[top:]
            pop_out_ref[slot, SUBSTEPS:, :] = kept[:top]

        @pl.when(slot >= own)
        def _():
            pop_out_ref[slot] = jnp.zeros((AGES, SIZES), jnp.float32)

    def arrive(item, carry):
        slot = target_of[item]
        inflow = scale_of[item] * state[item]
        pop_out_ref[slot, :SUBSTEPS, :] = pop_out_ref[slot, :SUBSTEPS, :] + inflow[top:]
        pop_out_ref[slot, SUBSTEPS:, :] = pop_out_ref[slot, SUBSTEPS:, :] + inflow[:top]
        return carry

    lax.fori_loop(0, total, arrive, 0)


def finish(swept, pos, table, lists, flow_rates, growth, daughter, turned, state, incoming):
    f32 = jnp.float32
    field = jax.ShapeDtypeStruct(pos.shape, f32)
    return pl.pallas_call(
        finish_kernel,
        out_shape=(field, field, jax.ShapeDtypeStruct((SLOTS, AGES, SIZES), f32)),
        in_specs=[VMEM_SPEC] * 3 + [SMEM_SPEC] * 2 + [VMEM_SPEC] * 4 + [HBM_SPEC],
        out_specs=(VMEM_SPEC,) * 3,
        scratch_shapes=[
            pltpu.VMEM((SLOTS + 1, AGES, SIZES), f32),
            pltpu.VMEM((SLOTS + 1, SIZES), f32),
            pltpu.VMEM((COLS, LANES), f32),
            pltpu.SMEM((COLS, LANES), f32),
            pltpu.SMEM((32,), f32),
            pltpu.SMEM((32,), f32),
            pltpu.SMEM((32,), f32),
            pltpu.SMEM((32,), jnp.int32),
            pltpu.SemaphoreType.DMA((1,)),
            pltpu.SemaphoreType.DMA,
        ],
        compiler_params=pltpu.CompilerParams(vmem_limit_bytes=VMEM_BYTES),
        cost_estimate=pl.CostEstimate(
            flops=2_000_000_000, bytes_accessed=8_000_000, transcendentals=0
        ),
    )(swept, pos, table, lists, flow_rates, growth, daughter, turned, state, incoming)


def per_device(
    substrate,
    oxygen,
    velocity,
    cell_map,
    owner_slot,
    flow_list,
    flow_rates,
    population,
    growth,
    daughter_kernel,
    division_rate,
    uptake_weight,
):
    owner = owner_slot.reshape(64, LANES)
    lists, payload = prepare(owner, flow_list, population)
    swept, pos, table, turned, state, incoming = sweep(
        substrate,
        oxygen,
        velocity,
        cell_map,
        owner,
        uptake_weight,
        growth,
        daughter_kernel,
        division_rate,
        population,
        payload,
    )
    return finish(
        swept, pos, table, lists, flow_rates, growth, daughter_kernel, turned, state, incoming
    )


def solution(mesh):
    return jax.shard_map(
        per_device,
        mesh=mesh,
        in_specs=(
            P("gz", "gx", "gy"),
            P("gz", "gx", "gy"),
            P(None, "gz", "gx", "gy"),
            P("gz", "gx", "gy"),
            P(),
            P(),
            P(),
            P(("gx", "gy", "gz"), None, None),
            P(),
            P(),
            P(),
            P(),
        ),
        out_specs=(P("gz", "gx", "gy"), P("gz", "gx", "gy"), P(("gx", "gy", "gz"), None, None)),
        check_vma=False,
    )
```

time: 121 us -> 100 us (0.83)
  the two profiles are of different devices: /device:TPU:35 before, /device:TPU:4 now
where the time goes in v2:
time: 100 us; the launch traced here: 99.6 us
  Pallas kernels  87.6 us (88%)
  local copies, waits for them, and re-layouts  11.3 us (11%)
    pallas_call x1, Pallas kernels, sweep(): pl.pallas_call(sweep_kernel, out_shape=(shape((2,) + sub.shape, f32), sha...  60.1 us
    pallas_call x1, Pallas kernels, finish(): pl.pallas_call(finish_kernel, out_shape=(field, field, jax.ShapeDtypeStru...  21.8 us
    unnamed x36, local copies, waits for them, and re-layouts  11.3 us
    pallas_call x1, Pallas kernels, prepare(): pl.pallas_call(prepare_kernel, out_shape=(jax.ShapeDtypeStruct((1, LANES)...  5.7 us

profile of v2, /device:TPU:4, one launch (start us, length us, event | category | flops | bytes accessed | tf_op | source)
XLA Modules:
  0.0 99.6 jit_solution(215123186965064765)
XLA Ops:
  0.6 0.0 copy-start
  0.6 1.6 %copy-done = f32[31,64,256]{2,1,0:T(8,128)S(1)} copy-done((f32[31,64,256]{2,1,0:T(8,128)S(1)}, f32[31,64,256]{2,1,0:T(8,128)}, u32[]{:S(2)}) %copy-start) | copy-done | bytes 2031640
  2.2 0.0 copy-start.2
  2.2 0.8 copy-done.2
  3.0 0.0 copy-start.3
  3.0 0.8 copy-done.3
  3.8 0.0 copy-start.4
  3.8 0.0 copy-start.11
  3.8 0.0 copy-start.15
  3.8 5.7 %shard_map.139 = (s32[1,128]{1,0:T(1,128)S(1)}, f32[16,128,256]{2,1,0:T(8,128)S(1)}) custom-call(s32[64,128]{1,0:T(8,128)S(1)} %bitcast.1, s32[2,8192]{1,0:T(2,128)S(1)} %copy-done.2, f32[31,64,256]{2,1,0:T(8,128)S(1)} %copy-done), custom_call_target="tpu_custom_call" | custom-call | flops 8000000 | bytes 6000000 | tf_op jit(solution)/shard_map/pallas_call | solution.py:138
  9.5 0.0 copy-start.5
  9.5 1.3 %copy-done.5 = f32[16,128,256]{2,1,0:T(8,128)} copy-done((f32[16,128,256]{2,1,0:T(8,128)}, f32[16,128,256]{2,1,0:T(8,128)S(1)}, u32[]{:S(2)}) %copy-start.5) | copy-done | bytes 2097176
  10.9 0.0 copy-done.1
  10.9 0.0 copy-done.4
  10.9 0.0 copy-done.11
  10.9 0.0 copy-done.15
  10.9 0.0 copy-start.6
  10.9 0.9 copy-done.6
  11.8 0.0 copy-start.7
  11.8 0.9 copy-done.7
  12.7 0.0 copy-start.9
  12.7 0.9 copy-done.9
  13.6 0.8 copy-done.12
  14.5 0.8 copy-done.13
  15.3 0.8 copy-done.14
  16.1 60.1 %shard_map.140 = (f32[2,4,32,128]{3,2,1,0:T(8,128)S(1)}, s32[4,32,128]{2,1,0:T(8,128)S(1)}, f32[16,16,128]{2,1,0:T(8,128)S(1)}, f32[8,64,256]{2,1,0:T(8,128)S(1)...) custom-call(f32[4,32,128]{2,1,0:T(8,128)S(1)} %copy-done.11, f32[4,32,128]{2,1,0:T(8,128)S(1)} %copy-done.12, ...), custom_call_target="tpu_custom_call" | custom-call | flops 3200000000 | bytes 8000000 | tf_op jit(solution)/shard_map/pallas_call | solution.py:536
  76.2 0.0 copy-done.8
  76.2 0.0 copy-done.10
  76.2 0.0 copy-done.16
  76.2 0.0 copy-start.17
  76.2 1.6 %copy-done.17 = f32[16,128,256]{2,1,0:T(8,128)S(1)} copy-done((f32[16,128,256]{2,1,0:T(8,128)S(1)}, f32[16,128,256]{2,1,0:T(8,128)}, u32[]{:S(2)}) %copy-start.17) | copy-done | bytes 2097176
  77.8 21.8 %shard_map.141 = (f32[4,32,128]{2,1,0:T(8,128)}, f32[4,32,128]{2,1,0:T(8,128)}, f32[31,64,256]{2,1,0:T(8,128)}) custom-call(f32[2,4,32,128]{3,2,1,0:T(8,128)S(1)} %get-tuple-element.12.swept_ref, s32[4,32,128]{2,1,0:T(8,128)S(1)} %get-tuple-element.13.pos_ref, f32[16,16,128]{2,1,0:T(8,128)S(1)} %get-tuple-element.14.table_ref, ...), custom_call_target="tpu_custom_call" | custom-call | flops 2000000000 | bytes 8000000 | tf_op jit(solution)/shard_map/pallas_call | solution.py:724
  (7 shorter events, 0.0 us)
Async XLA Ops:
  0.6 1.6 %copy-start = (f32[31,64,256]{2,1,0:T(8,128)S(1)}, f32[31,64,256]{2,1,0:T(8,128)}, u32[]{:S(2)}) copy-start(f32[31,64,256]{2,1,0:T(8,128)} %pop_ref.3) | copy-start | bytes 6094852
  2.2 0.8 copy-start.2
  3.0 0.8 copy-start.3
  3.8 7.1 %copy-start.1 = (f32[31,64,256]{2,1,0:T(8,128)S(1)}, f32[31,64,256]{2,1,0:T(8,128)}, u32[]{:S(2)}) copy-start(f32[31,64,256]{2,1,0:T(8,128)} %pop_ref.3) | copy-start | bytes 6094852
  3.8 7.1 %copy-start.4 = (s32[8192]{0:T(1024)S(1)}, s32[8192]{0:T(1024)}, u32[]{:S(2)}) copy-start(s32[8192]{0:T(1024)} %param.16) | copy-start | bytes 98308
  3.8 7.1 %copy-start.11 = (f32[4,32,128]{2,1,0:T(8,128)S(1)}, f32[4,32,128]{2,1,0:T(8,128)}, u32[]{:S(2)}) copy-start(f32[4,32,128]{2,1,0:T(8,128)} %sub_ref.1) | copy-start | bytes 196612
  3.8 7.1 %copy-start.15 = (f32[2,256]{1,0:T(2,128)S(1)}, f32[2,256]{1,0:T(2,128)}, u32[]{:S(2)}) copy-start(f32[2,256]{1,0:T(2,128)} %weight_ref.1) | copy-start | bytes 6148
  9.5 1.3 %copy-start.5 = (f32[16,128,256]{2,1,0:T(8,128)}, f32[16,128,256]{2,1,0:T(8,128)S(1)}, u32[]{:S(2)}) copy-start(f32[16,128,256]{2,1,0:T(8,128)S(1)} %get-tuple-element.11.payload_ref) | copy-start | bytes 6291460
  10.9 0.9 copy-start.6
  11.8 0.9 copy-start.7
  12.7 0.9 copy-start.9
  13.6 0.8 copy-start.12
  14.5 0.8 copy-start.13
  15.3 0.8 copy-start.14
  16.1 60.1 %copy-start.8 = (bf16[256,256]{1,0:T(8,128)(2,1)S(1)}, bf16[256,256]{1,0:T(8,128)(2,1)}, u32[]{:S(2)}) copy-start(bf16[256,256]{1,0:T(8,128)(2,1)} %growth_ref.3) | copy-start | bytes 393220
  16.1 60.1 %copy-start.10 = (bf16[256,256]{1,0:T(8,128)(2,1)S(1)}, bf16[256,256]{1,0:T(8,128)(2,1)}, u32[]{:S(2)}) copy-start(bf16[256,256]{1,0:T(8,128)(2,1)} %daughter_ref.3) | copy-start | bytes 393220
  16.1 60.1 %copy-start.16 = (f32[16]{0:T(128)S(1)}, f32[16]{0:T(128)}, u32[]{:S(2)}) copy-start(f32[16]{0:T(128)} %flow_rate_ref.1) | copy-start | bytes 196
  76.2 1.6 %copy-start.17 = (f32[16,128,256]{2,1,0:T(8,128)S(1)}, f32[16,128,256]{2,1,0:T(8,128)}, u32[]{:S(2)}) copy-start(f32[16,128,256]{2,1,0:T(8,128)} %get-tuple-element.18.incoming_ref) | copy-start | bytes 6291460

commit v3 on v2

--- a/solution.py
+++ b/solution.py
@@ -34,7 +34,7 @@
 VMEM_SPEC = pl.BlockSpec(memory_space=pltpu.VMEM)
 SMEM_SPEC = pl.BlockSpec(memory_space=pltpu.SMEM)
 HBM_SPEC = pl.BlockSpec(memory_space=pltpu.HBM)
-VMEM_BYTES = 48 * 1024 * 1024
+VMEM_BYTES = 66_900_000
 
 
 def iota(shape, dim):
@@ -51,37 +51,44 @@
     return jnp.where(high == row_id, found, total)
 
 
-def prepare_kernel(
-    owner_hbm,
-    flow_hbm,
-    pop_ref,
-    list_ref,
-    payload_ref,
-    owner_ref,
-    flow_ref,
-    target_ref,
-    index_ref,
-    row_ref,
-    list_smem,
-    load_sem,
-    list_sem,
-    pay_sem,
-):
-    column = lax.axis_index("gx") * 4 + lax.axis_index("gy")
-    me = column * DEPTH + lax.axis_index("gz")
-    loads = [
-        pltpu.make_async_copy(owner_hbm, owner_ref, load_sem.at[0]),
-        pltpu.make_async_copy(flow_hbm, flow_ref, load_sem.at[1]),
-    ]
-    for load in loads:
-        load.start()
-    for load in loads:
-        load.wait()
+def grow_rounds(state, rate_of, mother_ref, turned_ref, growth_ref, daughter_ref, groups):
+    for step in range(SUBSTEPS):
+        oldest = AGES - 1 - step
+
+        def one_group(group, carry, oldest=oldest, step=step):
+            base = group * GROUP
+            held = state[pl.ds(base, GROUP)]
+            moved = jnp.dot(
+                held.reshape(GROUP * AGES, SIZES).astype(jnp.bfloat16),
+                growth_ref[...],
+                preferred_element_type=jnp.float32,
+            ).reshape(GROUP, AGES, SIZES)
+            for slot in range(GROUP):
+                rate = rate_of(base + slot)
+                grown = held[slot] + rate * (moved[slot] - held[slot])
+                divided = (turned_ref[step] * rate) * grown
+                remain = grown - divided
+                mother_ref[pl.ds(base + slot, 1), :] = jnp.sum(divided, axis=0, keepdims=True)
+                state[base + slot] = remain
+                state[base + slot, oldest - 1 : oldest, :] = (
+                    remain[oldest - 1 : oldest, :] + remain[oldest : oldest + 1, :]
+                )
+            return carry
+
+        lax.fori_loop(0, groups, one_group, 0)
+        newborn = 2.0 * jnp.dot(
+            mother_ref[...].astype(jnp.bfloat16),
+            daughter_ref[...],
+            preferred_element_type=jnp.float32,
+        )
+        state[:, oldest, :] = newborn
+
+
+def list_flows(me, owner_ref, flow_ref, target_ref, index_ref, row_ref):
     for row in range(64):
         lanes = slice(row * LANES, (row + 1) * LANES)
         target_ref[row : row + 1, :] = flow_ref[0:1, lanes]
         index_ref[row : row + 1, :] = flow_ref[1:2, lanes]
-
     owner = owner_ref[...]
     targets = target_ref[...]
     low, high = targets & 127, targets >> 7
@@ -112,87 +119,37 @@
         is_low, jnp.min(rows, axis=1, keepdims=True), jnp.max(rows, axis=1, keepdims=True)
     )
     diagonal = jnp.where(iota(square, 0) == iota(square, 1), reduced, 0.0)
-    list_ref[...] = jnp.sum(diagonal, axis=0, keepdims=True).astype(jnp.int32)
-    to_scalar = pltpu.make_async_copy(list_ref, list_smem, list_sem)
-    to_scalar.start()
-    to_scalar.wait()
-    for col in range(COLS):
-        lowest, highest = list_smem[0, col], list_smem[0, col + 16]
-        first = jnp.where(highest >= 0, lowest >> 4, 0)
-        second = jnp.where(highest >= 0, highest >> 4, 0)
-        for rank, slot in enumerate((first, second)):
-            pltpu.make_async_copy(
-                pop_ref.at[slot],
-                payload_ref.at[col, pl.ds(rank * AGES, AGES)],
-                pay_sem.at[col * 2 + rank],
-            ).start()
-    for item in range(2 * COLS):
-        pltpu.make_async_copy(
-            pop_ref.at[0],
-            payload_ref.at[item // 2, pl.ds((item % 2) * AGES, AGES)],
-            pay_sem.at[item],
-        ).wait()
-
-
-def prepare(owner, flow, population):
-    return pl.pallas_call(
-        prepare_kernel,
-        out_shape=(
-            jax.ShapeDtypeStruct((1, LANES), jnp.int32),
-            jax.ShapeDtypeStruct((COLS, 2 * AGES, SIZES), jnp.float32),
-        ),
-        in_specs=[HBM_SPEC, HBM_SPEC, HBM_SPEC],
-        out_specs=(VMEM_SPEC, HBM_SPEC),
-        scratch_shapes=[
-            pltpu.VMEM((64, LANES), jnp.int32),
-            pltpu.VMEM(flow.shape, jnp.int32),
-            pltpu.VMEM((64, LANES), jnp.int32),
-            pltpu.VMEM((64, LANES), jnp.int32),
-            pltpu.VMEM((64, LANES), jnp.float32),
-            pltpu.SMEM((1, LANES), jnp.int32),
-            pltpu.SemaphoreType.DMA((2,)),
-            pltpu.SemaphoreType.DMA,
-            pltpu.SemaphoreType.DMA((2 * COLS,)),
-        ],
-        compiler_params=pltpu.CompilerParams(vmem_limit_bytes=16 * 1024 * 1024),
-        cost_estimate=pl.CostEstimate(flops=8_000_000, bytes_accessed=6_000_000, transcendentals=0),
-    )(owner, flow, population)
-
-
-def grow_rounds(state, rate_of, mother_ref, turned_ref, growth_ref, daughter_ref, groups):
-    for step in range(SUBSTEPS):
-        oldest = AGES - 1 - step
-
-        def one_group(group, carry, oldest=oldest, step=step):
-            base = group * GROUP
-            held = state[pl.ds(base, GROUP)]
-            moved = jnp.dot(
-                held.reshape(GROUP * AGES, SIZES).astype(jnp.bfloat16),
-                growth_ref[...],
-                preferred_element_type=jnp.float32,
-            ).reshape(GROUP, AGES, SIZES)
-            for slot in range(GROUP):
-                rate = rate_of(base + slot)
-                grown = held[slot] + rate * (moved[slot] - held[slot])
-                divided = (turned_ref[step] * rate) * grown
-                remain = grown - divided
-                mother_ref[pl.ds(base + slot, 1), :] = jnp.sum(divided, axis=0, keepdims=True)
-                state[base + slot] = remain
-                state[base + slot, oldest - 1 : oldest, :] = (
-                    remain[oldest - 1 : oldest, :] + remain[oldest : oldest + 1, :]
-                )
-            return carry
-
-        lax.fori_loop(0, groups, one_group, 0)
-        newborn = 2.0 * jnp.dot(
-            mother_ref[...].astype(jnp.bfloat16),
-            daughter_ref[...],
-            preferred_element_type=jnp.float32,
-        )
-        state[:, oldest, :] = newborn
+    return jnp.sum(diagonal, axis=0, keepdims=True).astype(jnp.int32)
 
 
 def sweep_kernel(
+    sub_hbm,
+    oxy_hbm,
+    vel_hbm,
+    map_hbm,
+    owner_hbm,
+    weight_hbm,
+    growth_hbm,
+    daughter_hbm,
+    division_hbm,
+    flow_hbm,
+    pop_ref,
+    fields_ref,
+    list_ref,
+    rates_ref,
+    turned_hbm,
+    state_hbm,
+    incoming_ref,
+    swept_ref,
+    pos_ref,
+    turned_ref,
+    state_ref,
+    payload_ref,
+    flow_ref,
+    target_ref,
+    index_ref,
+    row_ref,
+    list_smem,
     sub_ref,
     oxy_ref,
     vel_ref,
@@ -202,14 +159,6 @@
     growth_ref,
     daughter_ref,
     division_ref,
-    pop_ref,
-    payload_ref,
-    swept_ref,
-    pos_ref,
-    table_ref,
-    turned_ref,
-    state_ref,
-    incoming_ref,
     x_send,
     x_recv,
     y_send,
@@ -248,15 +197,29 @@
     same_core_ids = [(gx, gy, lax.rem(gz + step, DEPTH)) for step in range(2, DEPTH, 2)]
     sibling = (gx, gy, gz + 1 - 2 * core)
 
+    pairs = (
+        (sub_hbm, sub_ref),
+        (oxy_hbm, oxy_ref),
+        (map_hbm, map_ref),
+        (owner_hbm, owner_ref),
+        (weight_hbm, weight_ref),
+        (division_hbm, division_ref),
+        (vel_hbm, vel_ref),
+        (growth_hbm, growth_ref),
+        (daughter_hbm, daughter_ref),
+        (flow_hbm, flow_ref),
+    )
+    loads = [
+        pltpu.make_async_copy(source, target, local_sem.at[6 + number])
+        for number, (source, target) in enumerate(pairs)
+    ]
+    for copy in loads:
+        copy.start()
     barrier = pltpu.get_barrier_semaphore()
     for peer in col_ids + deep_ids:
         pl.semaphore_signal(barrier, inc=1, device_id=peer, device_id_type=MESH)
     load = pltpu.make_async_copy(pop_ref, state_ref.at[pl.ds(0, SLOTS)], local_sem.at[0])
     load.start()
-    stay = pltpu.make_async_copy(
-        payload_ref.at[column], incoming_ref.at[column], local_sem.at[1]
-    )
-    stay.start()
 
     def send(stage, ids, source_of, target):
         for number, device in enumerate(ids):
@@ -294,6 +257,8 @@
             copy.start()
             flows.append(copy)
 
+    for copy in loads[:2]:
+        copy.wait()
     fields = (sub_ref, oxy_ref)
     for field, ref in enumerate(fields):
         layers = slice(field * 4, field * 4 + 4)
@@ -303,52 +268,19 @@
         y_send[0, field : field + 1, :] = turned[0:1, :]
         y_send[1, field : field + 1, :] = turned[LANES - 1 : LANES, :]
 
+    for copy in loads[2:]:
+        copy.wait()
+    list_ref[...] = list_flows(
+        column * DEPTH + gz, owner_ref, flow_ref, target_ref, index_ref, row_ref
+    )
+    list_copy = pltpu.make_async_copy(list_ref, list_smem, local_sem.at[1])
+    list_copy.start()
     owner = owner_ref[...]
     owner_dev = device_of(owner)
     owner_local = owner - owner_dev * SLOTS
     place_ref[...] = (owner_dev >> 1) * 32 + jnp.where(
         (owner_dev & 1) == 1, 31 - owner_local, owner_local
     )
-    cells = map_ref[...].reshape(LANES, LANES)
-    low, high = cells & 127, cells >> 7
-
-    def find(step, total):
-        for part in range(8):
-            row = step * 8 + part
-            total = lookup(place_ref[pl.ds(row, 1), :], low, high, row, total)
-        return total
-
-    place = lax.fori_loop(0, 8, find, jnp.zeros_like(cells))
-    pos_ref[...] = place.reshape(pos_ref.shape)
-
-    division = division_ref[...]
-    turned_ref[0] = division
-    for step in range(1, SUBSTEPS):
-        turned_ref[step] = pltpu.roll(division, AGES - step, 0)
-
-    load.wait()
-    state_ref[SLOTS] = jnp.zeros((AGES, SIZES), jnp.float32)
-    for slot in range(SLOTS + 1):
-        ages_ref[slot : slot + 1, :] = jnp.sum(state_ref[slot], axis=0, keepdims=True)
-    summed = ages_ref[...]
-    owned = jnp.where(owner_dev == column * DEPTH + gz, 1.0, 0.0)
-    held = jnp.sum(jnp.sum(owned, axis=0, keepdims=True), axis=1, keepdims=True)
-    block = lax.rem(chip, 4)
-    wide = (DEPTH, LANES)
-    lane = iota(wide, 1)
-    local = lane & 31
-    slot_of_lane = jnp.where(core == 1, 31 - local, local)
-    here = ((lane >> 5) == block) & (slot_of_lane == iota(wide, 0))
-    here = here & (slot_of_lane.astype(jnp.float32) < held)
-    masses = []
-    for field in range(2):
-        weighted = summed * weight_ref[field : field + 1, :]
-        mass = jnp.sum(weighted, axis=1, keepdims=True) / (AGES * SIZES)
-        masses.append(jnp.sum(jnp.where(here, mass, 0.0), axis=0, keepdims=True))
-    packed = masses[0] + pltpu.roll(masses[1], 32, 1)
-    bio_send[0] = packed
-    bio_recv[gz] = packed
-
     pl.semaphore_wait(barrier, len(col_ids) + len(deep_ids))
 
     halos = []
@@ -378,7 +310,66 @@
             )
     for copy in halos:
         copy.start()
+
+    load.wait()
+    state_ref[SLOTS] = jnp.zeros((AGES, SIZES), jnp.float32)
+    for slot in range(SLOTS + 1):
+        ages_ref[slot : slot + 1, :] = jnp.sum(state_ref[slot], axis=0, keepdims=True)
+    summed = ages_ref[...]
+    owned = jnp.where(owner_dev == column * DEPTH + gz, 1.0, 0.0)
+    held = jnp.sum(jnp.sum(owned, axis=0, keepdims=True), axis=1, keepdims=True)
+    block = lax.rem(chip, 4)
+    wide = (DEPTH, LANES)
+    lane = iota(wide, 1)
+    local = lane & 31
+    slot_of_lane = jnp.where(core == 1, 31 - local, local)
+    here = ((lane >> 5) == block) & (slot_of_lane == iota(wide, 0))
+    here = here & (slot_of_lane.astype(jnp.float32) < held)
+    masses = []
+    for field in range(2):
+        weighted = summed * weight_ref[field : field + 1, :]
+        mass = jnp.sum(weighted, axis=1, keepdims=True) / (AGES * SIZES)
+        masses.append(jnp.sum(jnp.where(here, mass, 0.0), axis=0, keepdims=True))
+    packed = masses[0] + pltpu.roll(masses[1], 32, 1)
+    bio_send[0] = packed
+    bio_recv[gz] = packed
     send(0, deep_ids, lambda number: bio_send.at[0], bio_recv.at[gz])
+
+    list_copy.wait()
+
+    def pack(col, carry):
+        lowest, highest = list_smem[0, col], list_smem[0, col + 16]
+        first = jnp.where(highest >= 0, (lowest >> 4) & 31, 0)
+        second = jnp.where(highest >= 0, (highest >> 4) & 31, 0)
+        payload_ref[col, :AGES, :] = state_ref[first]
+        payload_ref[col, AGES:, :] = state_ref[second]
+        return carry
+
+    lax.fori_loop(0, COLS, pack, 0)
+    stay = pltpu.make_async_copy(
+        payload_ref.at[column], incoming_ref.at[column], local_sem.at[2]
+    )
+    stay.start()
+
+    cells = map_ref[...].reshape(LANES, LANES)
+    low, high = cells & 127, cells >> 7
+
+    def find(step, total):
+        for part in range(8):
+            row = step * 8 + part
+            total = lookup(place_ref[pl.ds(row, 1), :], low, high, row, total)
+        return total
+
+    place = lax.fori_loop(0, 8, find, jnp.zeros_like(cells))
+    pos_ref[...] = place.reshape(pos_ref.shape)
+
+    division = division_ref[...]
+    turned_ref[0] = division
+    for step in range(1, SUBSTEPS):
+        turned_ref[step] = pltpu.roll(division, AGES - step, 0)
+    turned_out = pltpu.make_async_copy(turned_ref, turned_hbm, local_sem.at[3])
+    turned_out.start()
+
     for copy in halos:
         copy.wait()
     send_flows(0)
@@ -491,7 +482,7 @@
     for row in range(4):
         own_row = own_row + jnp.where(gz // 8 == row, rate[row : row + 1, :], 0.0)
     rate_row[...] = own_row
-    to_scalar = pltpu.make_async_copy(rate_row, rate_smem, local_sem.at[2])
+    to_scalar = pltpu.make_async_copy(rate_row, rate_smem, local_sem.at[4])
     to_scalar.start()
 
     arrived(0, bio_recv, DEPTH - 1)
@@ -517,8 +508,35 @@
 
     grow_rounds(state_ref, rate_of, mother_ref, turned_ref, growth_ref, daughter_ref, 4)
 
+    state_out = pltpu.make_async_copy(state_ref, state_hbm, local_sem.at[5])
+    state_out.start()
+
     arrived(5, d_recv, COLS - 1)
-    table_ref[...] = d_recv[...]
+    rates = jnp.zeros((COLS, LANES), jnp.float32)
+    for row in range(4):
+        rates = rates + jnp.where(gz // 8 == row, d_recv[:, 8 + row, :], 0.0)
+    rates_ref[...] = rates
+
+    cells = pos_ref[...].reshape(LANES, LANES)
+    low, high = cells & 127, cells >> 7
+
+    def draw(col, drawn):
+        first, second = drawn
+        tile = d_recv[col]
+        for part in range(4):
+            row = col * 4 + part
+            first = lookup(tile[part : part + 1, :], low, high, row, first)
+            second = lookup(tile[4 + part : 5 + part, :], low, high, row, second)
+        return first, second
+
+    zero = jnp.zeros((LANES, LANES), jnp.float32)
+    drawn = lax.fori_loop(0, COLS, draw, (zero, zero))
+    for field, half in enumerate((half_substrate, half_oxygen)):
+        swept = swept_ref[field]
+        fields_ref[field] = swept - drawn[field].reshape(shape) * swept / (half + swept)
+
+    turned_out.wait()
+    state_out.wait()
     left_here(0, bio_recv, DEPTH - 1)
     left_here(1, a_recv, COLS - 1)
     left_here(2, pair_recv, 1)
@@ -530,22 +548,41 @@
         copy.wait()
 
 
-def sweep(sub, oxy, velocity, cell_map, owner, weight, growth, daughter, division, pop, payload):
+def sweep(sub, oxy, velocity, cell_map, owner, weight, growth, daughter, division, flow, pop):
     f32 = jnp.float32
     shape = jax.ShapeDtypeStruct
     return pl.pallas_call(
         sweep_kernel,
         out_shape=(
             shape((2,) + sub.shape, f32),
-            shape(sub.shape, jnp.int32),
-            shape((COLS, 16, LANES), f32),
+            shape((1, LANES), jnp.int32),
+            shape((COLS, LANES), f32),
             shape((SUBSTEPS, AGES, SIZES), f32),
             shape((SLOTS + 1, AGES, SIZES), f32),
-            shape(payload.shape, f32),
+            shape((COLS, 2 * AGES, SIZES), f32),
         ),
-        in_specs=[VMEM_SPEC] * 9 + [HBM_SPEC] * 2,
-        out_specs=(VMEM_SPEC,) * 5 + (HBM_SPEC,),
+        in_specs=[HBM_SPEC] * 11,
+        out_specs=(VMEM_SPEC,) * 3 + (HBM_SPEC,) * 3,
         scratch_shapes=[
+            pltpu.VMEM((2,) + sub.shape, f32),
+            pltpu.VMEM(sub.shape, jnp.int32),
+            pltpu.VMEM((SUBSTEPS, AGES, SIZES), f32),
+            pltpu.VMEM((SLOTS + 1, AGES, SIZES), f32),
+            pltpu.VMEM((COLS, 2 * AGES, SIZES), f32),
+            pltpu.VMEM(flow.shape, jnp.int32),
+            pltpu.VMEM((64, LANES), jnp.int32),
+            pltpu.VMEM((64, LANES), jnp.int32),
+            pltpu.VMEM((64, LANES), f32),
+            pltpu.SMEM((1, LANES), jnp.int32),
+            pltpu.VMEM(sub.shape, f32),
+            pltpu.VMEM(sub.shape, f32),
+            pltpu.VMEM(velocity.shape, f32),
+            pltpu.VMEM(sub.shape, jnp.int32),
+            pltpu.VMEM((64, LANES), jnp.int32),
+            pltpu.VMEM(weight.shape, f32),
+            pltpu.VMEM(growth.shape, growth.dtype),
+            pltpu.VMEM(daughter.shape, daughter.dtype),
+            pltpu.VMEM(division.shape, f32),
             pltpu.VMEM((2, 8, LANES), f32),
             pltpu.VMEM((2, 8, LANES), f32),
             pltpu.VMEM((2, 2, LANES), f32),
@@ -567,7 +604,7 @@
             pltpu.VMEM((COLS, 16, LANES), f32),
             pltpu.VMEM((1, LANES), f32),
             pltpu.SMEM((1, LANES), f32),
-            pltpu.SemaphoreType.DMA((3,)),
+            pltpu.SemaphoreType.DMA((16,)),
             pltpu.SemaphoreType.DMA((8,)),
             pltpu.SemaphoreType.DMA((8,)),
             pltpu.SemaphoreType.DMA((COLS - 1,)),
@@ -581,58 +618,52 @@
         cost_estimate=pl.CostEstimate(
             flops=3_200_000_000, bytes_accessed=8_000_000, transcendentals=0
         ),
-    )(sub, oxy, velocity, cell_map, owner, weight, growth, daughter, division, pop, payload)
+    )(sub, oxy, velocity, cell_map, owner, weight, growth, daughter, division, flow, pop)
 
 
 def finish_kernel(
-    swept_ref,
-    pos_ref,
-    table_ref,
     list_ref,
+    rate_table,
     flow_rate_ref,
-    growth_ref,
-    daughter_ref,
-    turned_ref,
-    own_ref,
+    fields_hbm,
+    own_hbm,
+    growth_hbm,
+    daughter_hbm,
+    turned_hbm,
     incoming_ref,
     sub_out_ref,
     oxy_out_ref,
     pop_out_ref,
+    own_ref,
+    growth_ref,
+    daughter_ref,
+    turned_ref,
     state,
     mother_ref,
-    rate_rows,
-    rate_table,
     rate_list,
     scale_of,
     own_scale,
     target_of,
+    load_sem,
     state_sem,
-    table_sem,
 ):
     depth = lax.axis_index("gz")
     core = depth & 1
     block = (depth >> 1) & 3
-    quarter = depth >> 3
-
-    rows = jnp.zeros((COLS, LANES), jnp.float32)
-    for part in range(4):
-        rows = rows + jnp.where(quarter == part, table_ref[:, 8 + part, :], 0.0)
-    rate_rows[...] = rows
-    to_scalar = pltpu.make_async_copy(rate_rows, rate_table, table_sem)
-    to_scalar.start()
-    to_scalar.wait()
-
-    def scan_own(col, count):
-        lowest, highest = list_ref[0, col], list_ref[0, col + 16]
-
-        @pl.when(highest >= 0)
-        def _():
-            own_scale[lowest >> 4] = flow_rate_ref[lowest & 15]
-            own_scale[highest >> 4] = flow_rate_ref[highest & 15]
-
-        return count + jnp.where(highest >= 0, 1, 0) + jnp.where(highest > lowest, 1, 0)
-
-    own = lax.fori_loop(0, COLS, scan_own, jnp.int32(0))
+    pairs = (
+        (own_hbm, own_ref),
+        (growth_hbm, growth_ref),
+        (daughter_hbm, daughter_ref),
+        (turned_hbm, turned_ref),
+        (fields_hbm.at[0], sub_out_ref),
+        (fields_hbm.at[1], oxy_out_ref),
+    )
+    loads = [
+        pltpu.make_async_copy(source, target, load_sem.at[number])
+        for number, (source, target) in enumerate(pairs)
+    ]
+    for copy in loads:
+        copy.start()
 
     def scan_arriving(item, count):
         col, rank = item >> 1, item & 1
@@ -657,25 +688,33 @@
 
     total = lax.fori_loop(0, 2 * COLS, scan_arriving, jnp.int32(0))
 
-    cells = pos_ref[...].reshape(LANES, LANES)
-    low, high = cells & 127, cells >> 7
-
-    def find(col, drawn):
-        first, second = drawn
-        tile = table_ref[col]
-        for part in range(4):
-            row = col * 4 + part
-            first = lookup(tile[part : part + 1, :], low, high, row, first)
-            second = lookup(tile[4 + part : 5 + part, :], low, high, row, second)
-        return first, second
-
-    zero = jnp.zeros((LANES, LANES), jnp.float32)
-    drawn = lax.fori_loop(0, COLS, find, (zero, zero))
-    for field, (out, half) in enumerate(
-        ((sub_out_ref, half_substrate), (oxy_out_ref, half_oxygen))
-    ):
-        swept = swept_ref[field]
-        out[...] = swept - drawn[field].reshape(swept.shape) * swept / (half + swept)
+    def scan_own(col, count):
+        lowest, highest = list_ref[0, col], list_ref[0, col + 16]
+
+        @pl.when(highest >= 0)
+        def _():
+            own_scale[lowest >> 4] = flow_rate_ref[lowest & 15]
+            own_scale[highest >> 4] = flow_rate_ref[highest & 15]
+
+        return count + jnp.where(highest >= 0, 1, 0) + jnp.where(highest > lowest, 1, 0)
+
+    own = lax.fori_loop(0, COLS, scan_own, jnp.int32(0))
+    for copy in loads:
+        copy.wait()
+
+    top = AGES - SUBSTEPS
+    for slot in range(SLOTS):
+
+        @pl.when(slot < own)
+        def _():
+            kept = own_ref[slot]
+            kept = kept - own_scale[slot] * kept
+            pop_out_ref[slot, :SUBSTEPS, :] = kept[top:]
+            pop_out_ref[slot, SUBSTEPS:, :] = kept[:top]
+
+        @pl.when(slot >= own)
+        def _():
+            pop_out_ref[slot] = jnp.zeros((AGES, SIZES), jnp.float32)
 
     def fetched(slot, carry):
         pltpu.make_async_copy(
@@ -694,20 +733,6 @@
         (total + GROUP - 1) // GROUP,
     )
 
-    top = AGES - SUBSTEPS
-    for slot in range(SLOTS):
-
-        @pl.when(slot < own)
-        def _():
-            kept = own_ref[slot]
-            kept = kept - own_scale[slot] * kept
-            pop_out_ref[slot, :SUBSTEPS, :] = kept[top:]
-            pop_out_ref[slot, SUBSTEPS:, :] = kept[:top]
-
-        @pl.when(slot >= own)
-        def _():
-            pop_out_ref[slot] = jnp.zeros((AGES, SIZES), jnp.float32)
-
     def arrive(item, carry):
         slot = target_of[item]
         inflow = scale_of[item] * state[item]
@@ -718,31 +743,33 @@
     lax.fori_loop(0, total, arrive, 0)
 
 
-def finish(swept, pos, table, lists, flow_rates, growth, daughter, turned, state, incoming):
+def finish(lists, rates, flow_rates, fields, state, growth, daughter, turned, incoming):
     f32 = jnp.float32
-    field = jax.ShapeDtypeStruct(pos.shape, f32)
+    field = jax.ShapeDtypeStruct(fields.shape[1:], f32)
     return pl.pallas_call(
         finish_kernel,
         out_shape=(field, field, jax.ShapeDtypeStruct((SLOTS, AGES, SIZES), f32)),
-        in_specs=[VMEM_SPEC] * 3 + [SMEM_SPEC] * 2 + [VMEM_SPEC] * 4 + [HBM_SPEC],
+        in_specs=[SMEM_SPEC] * 3 + [HBM_SPEC] * 6,
         out_specs=(VMEM_SPEC,) * 3,
         scratch_shapes=[
+            pltpu.VMEM(state.shape, f32),
+            pltpu.VMEM(growth.shape, growth.dtype),
+            pltpu.VMEM(daughter.shape, daughter.dtype),
+            pltpu.VMEM(turned.shape, f32),
             pltpu.VMEM((SLOTS + 1, AGES, SIZES), f32),
             pltpu.VMEM((SLOTS + 1, SIZES), f32),
-            pltpu.VMEM((COLS, LANES), f32),
-            pltpu.SMEM((COLS, LANES), f32),
             pltpu.SMEM((32,), f32),
             pltpu.SMEM((32,), f32),
             pltpu.SMEM((32,), f32),
             pltpu.SMEM((32,), jnp.int32),
+            pltpu.SemaphoreType.DMA((6,)),
             pltpu.SemaphoreType.DMA((1,)),
-            pltpu.SemaphoreType.DMA,
         ],
         compiler_params=pltpu.CompilerParams(vmem_limit_bytes=VMEM_BYTES),
         cost_estimate=pl.CostEstimate(
             flops=2_000_000_000, bytes_accessed=8_000_000, transcendentals=0
         ),
-    )(swept, pos, table, lists, flow_rates, growth, daughter, turned, state, incoming)
+    )(lists, rates, flow_rates, fields, state, growth, daughter, turned, incoming)
 
 
 def per_device(
@@ -759,23 +786,21 @@
     division_rate,
     uptake_weight,
 ):
-    owner = owner_slot.reshape(64, LANES)
-    lists, payload = prepare(owner, flow_list, population)
-    swept, pos, table, turned, state, incoming = sweep(
+    fields, lists, rates, turned, state, incoming = sweep(
         substrate,
         oxygen,
         velocity,
         cell_map,
-        owner,
+        owner_slot.reshape(64, LANES),
         uptake_weight,
         growth,
         daughter_kernel,
         division_rate,
+        flow_list,
         population,
-        payload,
     )
     return finish(
-        swept, pos, table, lists, flow_rates, growth, daughter_kernel, turned, state, incoming
+        lists, rates, flow_rates, fields, state, growth, daughter_kernel, turned, incoming
     )
 
 

time: 100 us -> 75.1 us (0.75)
  the two profiles are of different devices: /device:TPU:4 before, /device:TPU:2 now
where the time goes in v3:
time: 75.1 us; the launch traced here: 74.9 us
  Pallas kernels  74.2 us (99%)
    pallas_call x1, Pallas kernels, sweep(): pl.pallas_call(sweep_kernel, out_shape=(shape((2,) + sub.shape, f32), sha...  60.8 us
    pallas_call x1, Pallas kernels, finish(): pl.pallas_call(finish_kernel, out_shape=(field, field, jax.ShapeDtypeStru...  13.5 us

profile of v3, /device:TPU:2, one launch (start us, length us, event | category | flops | bytes accessed | tf_op | source)
XLA Modules:
  0.0 74.9 jit_solution(7605786562417278400)
XLA Ops:
  0.6 60.8 %shard_map.139 = (f32[2,4,32,128]{3,2,1,0:T(8,128)}, s32[1,128]{1,0:T(1,128)}, f32[16,128]{1,0:T(8,128)}, f32[8,64,256]{2,1,0:T(8,128)}, f32[32,64,256]{2,1,0:T(8,128)}, /*index=5*/f32[16,128,256]{2,1,0:T(8,128)}) custom-call(f32[4,32,128]{2,1,0:T(8,128)} %sub_hbm.1, f32[4,32,128]{2,1,0:T(8,128)} %oxy_hbm.1, f32[3,4,32,128]{3,2,1,0:T(8,128)} %vel_hbm.1, ...), custom_call_target="tpu_custom_call" | custom-call | flops 3200000000 | bytes 8000000 | tf_op jit(solution)/shard_map/pallas_call | solution.py:554
  61.4 13.5 %shard_map.140 = (f32[4,32,128]{2,1,0:T(8,128)}, f32[4,32,128]{2,1,0:T(8,128)}, f32[31,64,256]{2,1,0:T(8,128)}) custom-call(s32[1,128]{1,0:T(1,128)} %get-tuple-element.9.list_ref, f32[16,128]{1,0:T(8,128)} %get-tuple-element.10.rate_table, f32[16]{0:T(128)} %flow_rate_ref.1, f32[2,4,32,128]{3,2,1,0:T(8,128)} %get-tuple-element.11.fields_hbm, ...), custom_call_target="tpu_custom_call" | custom-call | flops 2000000000 | bytes 8000000 | tf_op jit(solution)/shard_map/pallas_call | solution.py:749

commit v4 on v3

--- a/solution.py
+++ b/solution.py
@@ -25,9 +25,9 @@
 uptake_gain = 3.0
 
 FLOW_PARTS = (
-    ((1, 0), (3, 0), (0, 1), (0, 3)),
-    ((2, 0), (0, 2), (1, 1), (3, 3), (1, 3), (3, 1)),
-    ((1, 2), (2, 1), (2, 3), (3, 2), (2, 2)),
+    ((1, 0), (3, 0), (0, 1), (0, 3), (2, 0), (0, 2)),
+    ((1, 1), (3, 3), (1, 3), (3, 1), (1, 2)),
+    ((2, 1), (2, 3), (3, 2), (2, 2)),
 )
 
 MESH = pl.DeviceIdType.MESH
@@ -312,29 +312,6 @@
         copy.start()
 
     load.wait()
-    state_ref[SLOTS] = jnp.zeros((AGES, SIZES), jnp.float32)
-    for slot in range(SLOTS + 1):
-        ages_ref[slot : slot + 1, :] = jnp.sum(state_ref[slot], axis=0, keepdims=True)
-    summed = ages_ref[...]
-    owned = jnp.where(owner_dev == column * DEPTH + gz, 1.0, 0.0)
-    held = jnp.sum(jnp.sum(owned, axis=0, keepdims=True), axis=1, keepdims=True)
-    block = lax.rem(chip, 4)
-    wide = (DEPTH, LANES)
-    lane = iota(wide, 1)
-    local = lane & 31
-    slot_of_lane = jnp.where(core == 1, 31 - local, local)
-    here = ((lane >> 5) == block) & (slot_of_lane == iota(wide, 0))
-    here = here & (slot_of_lane.astype(jnp.float32) < held)
-    masses = []
-    for field in range(2):
-        weighted = summed * weight_ref[field : field + 1, :]
-        mass = jnp.sum(weighted, axis=1, keepdims=True) / (AGES * SIZES)
-        masses.append(jnp.sum(jnp.where(here, mass, 0.0), axis=0, keepdims=True))
-    packed = masses[0] + pltpu.roll(masses[1], 32, 1)
-    bio_send[0] = packed
-    bio_recv[gz] = packed
-    send(0, deep_ids, lambda number: bio_send.at[0], bio_recv.at[gz])
-
     list_copy.wait()
 
     def pack(col, carry):
@@ -350,6 +327,7 @@
         payload_ref.at[column], incoming_ref.at[column], local_sem.at[2]
     )
     stay.start()
+    send_flows(0)
 
     cells = map_ref[...].reshape(LANES, LANES)
     low, high = cells & 127, cells >> 7
@@ -363,16 +341,8 @@
     place = lax.fori_loop(0, 8, find, jnp.zeros_like(cells))
     pos_ref[...] = place.reshape(pos_ref.shape)
 
-    division = division_ref[...]
-    turned_ref[0] = division
-    for step in range(1, SUBSTEPS):
-        turned_ref[step] = pltpu.roll(division, AGES - step, 0)
-    turned_out = pltpu.make_async_copy(turned_ref, turned_hbm, local_sem.at[3])
-    turned_out.start()
-
     for copy in halos:
         copy.wait()
-    send_flows(0)
 
     shape = (4, 32, LANES)
     row_id = iota(shape, 1)
@@ -411,26 +381,44 @@
         swept_ref[field] = total
         value_ref[field] = total.reshape(LANES, LANES)
 
-    fine_row = iota((2 * LANES, LANES), 0)
-    sub_row = iota((64, LANES), 0)
-    row_half = sub_row >> 1
-    even = (sub_row & 1) == 0
+    bf16 = jnp.bfloat16
+
+    def small(values):
+        return values.astype(jnp.float32).astype(bf16)
+
+    fine_row = small(iota((2 * LANES, LANES), 0))
+    row_half = small(iota((64, LANES), 0) >> 1)
+    even = (iota((16, LANES), 0) & 1) == 0
 
     def gather_sums(step, total):
         rows = pl.ds(pl.multiple_of(step * 8, 8), 8)
         place = pos_ref[step // 4, pl.ds(pl.multiple_of(lax.rem(step, 4) * 8, 8), 8), :]
+        coarse_place = (place >> 8).astype(jnp.float32)
+        fine_place = (place & 255).astype(jnp.float32)
         first = value_ref[0, rows, :]
         second = value_ref[1, rows, :]
         left, right = [], []
         for row in range(8):
             one = slice(row, row + 1)
             value = jnp.where(even, first[one], second[one])
-            coarse = value.astype(jnp.bfloat16).astype(jnp.float32)
-            hit = (place[one] >> 8) == row_half
-            top = jnp.where(hit, coarse, 0.0).astype(jnp.bfloat16)
-            rest = jnp.where(hit, value - coarse, 0.0).astype(jnp.bfloat16)
-            left.append(jnp.concatenate([top, rest], axis=0))
-            right.append(jnp.where((place[one] & 255) == fine_row, 1.0, 0.0).astype(jnp.bfloat16))
+            coarse = value.astype(bf16)
+            rest = (value - coarse.astype(jnp.float32)).astype(bf16)
+            tall = jnp.broadcast_to(coarse_place[one], (16, LANES)).astype(bf16)
+            hit = jnp.concatenate([tall] * 4, axis=0) == row_half
+            zero = jnp.zeros((64, LANES), bf16)
+            left.append(
+                jnp.concatenate(
+                    [
+                        jnp.where(hit, jnp.concatenate([coarse] * 4, axis=0), zero),
+                        jnp.where(hit, jnp.concatenate([rest] * 4, axis=0), zero),
+                    ],
+                    axis=0,
+                )
+            )
+            tall = jnp.broadcast_to(fine_place[one], (16, LANES)).astype(bf16)
+            hit = jnp.concatenate([tall] * 16, axis=0) == fine_row
+            ones = jnp.ones((2 * LANES, LANES), bf16)
+            right.append(jnp.where(hit, ones, jnp.zeros_like(ones)))
         return total + lax.dot_general(
             jnp.concatenate(left, axis=1),
             jnp.concatenate(right, axis=1),
@@ -443,6 +431,37 @@
 
     send(1, col_ids, lambda number: sums_ref.at[col_peers[number]], a_recv.at[column])
     a_recv[column] = sums_ref[column]
+
+    state_ref[SLOTS] = jnp.zeros((AGES, SIZES), jnp.float32)
+    for slot in range(SLOTS + 1):
+        ages_ref[slot : slot + 1, :] = jnp.sum(state_ref[slot], axis=0, keepdims=True)
+    summed = ages_ref[...]
+    owned = jnp.where(owner_dev == column * DEPTH + gz, 1.0, 0.0)
+    held = jnp.sum(jnp.sum(owned, axis=0, keepdims=True), axis=1, keepdims=True)
+    block = lax.rem(chip, 4)
+    wide = (DEPTH, LANES)
+    lane = iota(wide, 1)
+    local = lane & 31
+    slot_of_lane = jnp.where(core == 1, 31 - local, local)
+    here = ((lane >> 5) == block) & (slot_of_lane == iota(wide, 0))
+    here = here & (slot_of_lane.astype(jnp.float32) < held)
+    masses = []
+    for field in range(2):
+        weighted = summed * weight_ref[field : field + 1, :]
+        mass = jnp.sum(weighted, axis=1, keepdims=True) / (AGES * SIZES)
+        masses.append(jnp.sum(jnp.where(here, mass, 0.0), axis=0, keepdims=True))
+    packed = masses[0] + pltpu.roll(masses[1], 32, 1)
+    bio_send[0] = packed
+    bio_recv[gz] = packed
+    send(0, deep_ids, lambda number: bio_send.at[0], bio_recv.at[gz])
+
+    division = division_ref[...]
+    turned_ref[0] = division
+    for step in range(1, SUBSTEPS):
+        turned_ref[step] = pltpu.roll(division, AGES - step, 0)
+    turned_out = pltpu.make_async_copy(turned_ref, turned_hbm, local_sem.at[3])
+    turned_out.start()
+
     arrived(1, a_recv, COLS - 1)
     send_flows(1)
     part = jnp.sum(a_recv[...], axis=0)
@@ -517,23 +536,58 @@
         rates = rates + jnp.where(gz // 8 == row, d_recv[:, 8 + row, :], 0.0)
     rates_ref[...] = rates
 
-    cells = pos_ref[...].reshape(LANES, LANES)
-    low, high = cells & 127, cells >> 7
-
-    def draw(col, drawn):
-        first, second = drawn
-        tile = d_recv[col]
-        for part in range(4):
-            row = col * 4 + part
-            first = lookup(tile[part : part + 1, :], low, high, row, first)
-            second = lookup(tile[4 + part : 5 + part, :], low, high, row, second)
-        return first, second
-
-    zero = jnp.zeros((LANES, LANES), jnp.float32)
-    drawn = lax.fori_loop(0, COLS, draw, (zero, zero))
+    tables = []
+    for field in range(2):
+        for half in range(2):
+            tables.append(
+                jnp.concatenate(
+                    [
+                        d_recv[:, field * 4 + 2 * half, :],
+                        d_recv[:, field * 4 + 2 * half + 1, :],
+                    ],
+                    axis=1,
+                )
+            )
+    whole = jnp.concatenate(tables, axis=0)
+    coarse_table = whole.astype(bf16)
+    rest_table = (whole - coarse_table.astype(jnp.float32)).astype(bf16)
+    both = jnp.concatenate([coarse_table, rest_table], axis=0)
+    table_row = iota((COLS, LANES), 0)
+
+    def draw(step, carry):
+        rows = pl.ds(pl.multiple_of(step * 8, 8), 8)
+        place = pos_ref[step // 4, pl.ds(pl.multiple_of(lax.rem(step, 4) * 8, 8), 8), :]
+        fine_place = (place & 255).astype(jnp.float32)
+        right = []
+        for row in range(8):
+            tall = jnp.broadcast_to(fine_place[row : row + 1], (16, LANES)).astype(bf16)
+            hit = jnp.concatenate([tall] * 16, axis=0) == fine_row
+            ones = jnp.ones((2 * LANES, LANES), bf16)
+            right.append(jnp.where(hit, ones, jnp.zeros_like(ones)))
+        found = jnp.dot(
+            both, jnp.concatenate(right, axis=1), preferred_element_type=jnp.float32
+        )
+        found = found[:64] + found[64:]
+        first, second = [], []
+        for row in range(8):
+            lanes = slice(row * LANES, (row + 1) * LANES)
+            high = place[row : row + 1] >> 8
+            for field, out in enumerate((first, second)):
+                kept = jnp.zeros((COLS, LANES), jnp.float32)
+                for half in range(2):
+                    at = (field * 2 + half) * COLS
+                    hit = high == 2 * table_row + half
+                    kept = kept + jnp.where(hit, found[at : at + COLS, lanes], 0.0)
+                out.append(jnp.sum(kept, axis=0, keepdims=True))
+        value_ref[0, rows, :] = jnp.concatenate(first, axis=0)
+        value_ref[1, rows, :] = jnp.concatenate(second, axis=0)
+        return carry
+
+    lax.fori_loop(0, 16, draw, 0)
     for field, half in enumerate((half_substrate, half_oxygen)):
         swept = swept_ref[field]
-        fields_ref[field] = swept - drawn[field].reshape(shape) * swept / (half + swept)
+        drawn = value_ref[field].reshape(shape)
+        fields_ref[field] = swept - drawn * swept / (half + swept)
 
     turned_out.wait()
     state_out.wait()

time: 75.1 us -> 72.3 us (0.963)
  Pallas kernels: 74.2 us -> 71.5 us
    pallas_call x1, Pallas kernels: 60.8 us -> 58 us  [sweep(): pl.pallas_call(sweep_kernel, out_shape=(shape((2,) + sub.shape, f32), sha...]
where the time goes in v4:
time: 72.3 us; the launch traced here: 72.1 us
  Pallas kernels  71.5 us (99%)
    pallas_call x1, Pallas kernels, sweep(): pl.pallas_call(sweep_kernel, out_shape=(shape((2,) + sub.shape, f32), sha...  58 us
    pallas_call x1, Pallas kernels, finish(): pl.pallas_call(finish_kernel, out_shape=(field, field, jax.ShapeDtypeStru...  13.5 us

profile of v4, /device:TPU:2, one launch (start us, length us, event | category | flops | bytes accessed | tf_op | source)
XLA Modules:
  0.0 72.1 jit_solution(15089400410725744994)
XLA Ops:
  0.6 58.0 %shard_map.139 = (f32[2,4,32,128]{3,2,1,0:T(8,128)}, s32[1,128]{1,0:T(1,128)}, f32[16,128]{1,0:T(8,128)}, f32[8,64,256]{2,1,0:T(8,128)}, f32[32,64,256]{2,1,0:T(8,128)}, /*index=5*/f32[16,128,256]{2,1,0:T(8,128)}) custom-call(f32[4,32,128]{2,1,0:T(8,128)} %sub_hbm.1, f32[4,32,128]{2,1,0:T(8,128)} %oxy_hbm.1, f32[3,4,32,128]{3,2,1,0:T(8,128)} %vel_hbm.1, ...), custom_call_target="tpu_custom_call" | custom-call | flops 3200000000 | bytes 8000000 | tf_op jit(solution)/shard_map/pallas_call | solution.py:608
  58.6 13.5 %shard_map.140 = (f32[4,32,128]{2,1,0:T(8,128)}, f32[4,32,128]{2,1,0:T(8,128)}, f32[31,64,256]{2,1,0:T(8,128)}) custom-call(s32[1,128]{1,0:T(1,128)} %get-tuple-element.9.list_ref, f32[16,128]{1,0:T(8,128)} %get-tuple-element.10.rate_table, f32[16]{0:T(128)} %flow_rate_ref.1, f32[2,4,32,128]{3,2,1,0:T(8,128)} %get-tuple-element.11.fields_hbm, ...), custom_call_target="tpu_custom_call" | custom-call | flops 2000000000 | bytes 8000000 | tf_op jit(solution)/shard_map/pallas_call | solution.py:803

commit v5 on v4

--- a/solution.py
+++ b/solution.py
@@ -26,8 +26,8 @@
 
 FLOW_PARTS = (
     ((1, 0), (3, 0), (0, 1), (0, 3), (2, 0), (0, 2)),
-    ((1, 1), (3, 3), (1, 3), (3, 1), (1, 2)),
-    ((2, 1), (2, 3), (3, 2), (2, 2)),
+    ((1, 1), (3, 3), (1, 3), (3, 1), (1, 2), (2, 1)),
+    ((2, 3), (3, 2), (2, 2)),
 )
 
 MESH = pl.DeviceIdType.MESH
@@ -51,19 +51,21 @@
     return jnp.where(high == row_id, found, total)
 
 
-def grow_rounds(state, rate_of, mother_ref, turned_ref, growth_ref, daughter_ref, groups):
+def grow_rounds(
+    state, rate_of, mother_ref, turned_ref, growth_ref, daughter_ref, groups, size
+):
     for step in range(SUBSTEPS):
         oldest = AGES - 1 - step
 
         def one_group(group, carry, oldest=oldest, step=step):
-            base = group * GROUP
-            held = state[pl.ds(base, GROUP)]
+            base = group * size
+            held = state[pl.ds(base, size)]
             moved = jnp.dot(
-                held.reshape(GROUP * AGES, SIZES).astype(jnp.bfloat16),
+                held.reshape(size * AGES, SIZES).astype(jnp.bfloat16),
                 growth_ref[...],
                 preferred_element_type=jnp.float32,
-            ).reshape(GROUP, AGES, SIZES)
-            for slot in range(GROUP):
+            ).reshape(size, AGES, SIZES)
+            for slot in range(size):
                 rate = rate_of(base + slot)
                 grown = held[slot] + rate * (moved[slot] - held[slot])
                 divided = (turned_ref[step] * rate) * grown
@@ -329,17 +331,41 @@
     stay.start()
     send_flows(0)
 
-    cells = map_ref[...].reshape(LANES, LANES)
-    low, high = cells & 127, cells >> 7
-
-    def find(step, total):
-        for part in range(8):
-            row = step * 8 + part
-            total = lookup(place_ref[pl.ds(row, 1), :], low, high, row, total)
-        return total
-
-    place = lax.fori_loop(0, 8, find, jnp.zeros_like(cells))
-    pos_ref[...] = place.reshape(pos_ref.shape)
+    bf16 = jnp.bfloat16
+
+    def small(values):
+        return values.astype(jnp.float32).astype(bf16)
+
+    fine_row = small(iota((2 * LANES, LANES), 0))
+    places = jnp.concatenate(
+        [place_ref[pl.ds(0, 32, stride=2), :], place_ref[pl.ds(1, 32, stride=2), :]], axis=1
+    )
+    pieces = jnp.concatenate([small(places & ~127), small(places & 127)], axis=0)
+    piece_row = iota((32, LANES), 0)
+
+    def find(step, carry):
+        rows = pl.ds(pl.multiple_of(lax.rem(step, 4) * 8, 8), 8)
+        cells = map_ref[step // 4, rows, :]
+        fine_cell = (cells & 255).astype(jnp.float32)
+        right = []
+        for row in range(8):
+            tall = jnp.broadcast_to(fine_cell[row : row + 1], (16, LANES)).astype(bf16)
+            hit = jnp.concatenate([tall] * 16, axis=0) == fine_row
+            ones = jnp.ones((2 * LANES, LANES), bf16)
+            right.append(jnp.where(hit, ones, jnp.zeros_like(ones)))
+        found = jnp.dot(
+            pieces, jnp.concatenate(right, axis=1), preferred_element_type=jnp.float32
+        )
+        found = found[:32] + found[32:]
+        lines = []
+        for row in range(8):
+            hit = (cells[row : row + 1] >> 8) == piece_row
+            kept = jnp.where(hit, found[:, row * LANES : (row + 1) * LANES], 0.0)
+            lines.append(jnp.sum(kept, axis=0, keepdims=True))
+        pos_ref[step // 4, rows, :] = jnp.concatenate(lines, axis=0).astype(jnp.int32)
+        return carry
+
+    lax.fori_loop(0, 16, find, 0)
 
     for copy in halos:
         copy.wait()
@@ -381,12 +407,6 @@
         swept_ref[field] = total
         value_ref[field] = total.reshape(LANES, LANES)
 
-    bf16 = jnp.bfloat16
-
-    def small(values):
-        return values.astype(jnp.float32).astype(bf16)
-
-    fine_row = small(iota((2 * LANES, LANES), 0))
     row_half = small(iota((64, LANES), 0) >> 1)
     even = (iota((16, LANES), 0) & 1) == 0
 
@@ -525,7 +545,7 @@
     def rate_of(slot):
         return rate_smem[0, block * 32 + jnp.where(core == 1, 31 - slot, slot)]
 
-    grow_rounds(state_ref, rate_of, mother_ref, turned_ref, growth_ref, daughter_ref, 4)
+    grow_rounds(state_ref, rate_of, mother_ref, turned_ref, growth_ref, daughter_ref, 2, 16)
 
     state_out = pltpu.make_async_copy(state_ref, state_hbm, local_sem.at[5])
     state_out.start()
@@ -785,6 +805,7 @@
         growth_ref,
         daughter_ref,
         (total + GROUP - 1) // GROUP,
+        GROUP,
     )
 
     def arrive(item, carry):

time: 72.3 us -> 70.4 us (0.974)
  the two profiles are of different devices: /device:TPU:2 before, /device:TPU:8 now
where the time goes in v5:
time: 70.4 us; the launch traced here: 69.6 us
  Pallas kernels  69 us (98%)
    pallas_call x1, Pallas kernels, sweep(): pl.pallas_call(sweep_kernel, out_shape=(shape((2,) + sub.shape, f32), sha...  55.6 us
    pallas_call x1, Pallas kernels, finish(): pl.pallas_call(finish_kernel, out_shape=(field, field, jax.ShapeDtypeStru...  13.4 us

profile of v5, /device:TPU:8, one launch (start us, length us, event | category | flops | bytes accessed | tf_op | source)
XLA Modules:
  0.0 69.6 jit_solution(17342659432092628569)
XLA Ops:
  0.6 55.6 %shard_map.139 = (f32[2,4,32,128]{3,2,1,0:T(8,128)}, s32[1,128]{1,0:T(1,128)}, f32[16,128]{1,0:T(8,128)}, f32[8,64,256]{2,1,0:T(8,128)}, f32[32,64,256]{2,1,0:T(8,128)}, /*index=5*/f32[16,128,256]{2,1,0:T(8,128)}) custom-call(f32[4,32,128]{2,1,0:T(8,128)} %sub_hbm.1, f32[4,32,128]{2,1,0:T(8,128)} %oxy_hbm.1, f32[3,4,32,128]{3,2,1,0:T(8,128)} %vel_hbm.1, ...), custom_call_target="tpu_custom_call" | custom-call | flops 3200000000 | bytes 8000000 | tf_op jit(solution)/shard_map/pallas_call | solution.py:628
  56.3 13.4 %shard_map.140 = (f32[4,32,128]{2,1,0:T(8,128)}, f32[4,32,128]{2,1,0:T(8,128)}, f32[31,64,256]{2,1,0:T(8,128)}) custom-call(s32[1,128]{1,0:T(1,128)} %get-tuple-element.9.list_ref, f32[16,128]{1,0:T(8,128)} %get-tuple-element.10.rate_table, f32[16]{0:T(128)} %flow_rate_ref.1, f32[2,4,32,128]{3,2,1,0:T(8,128)} %get-tuple-element.11.fields_hbm, ...), custom_call_target="tpu_custom_call" | custom-call | flops 2000000000 | bytes 8000000 | tf_op jit(solution)/shard_map/pallas_call | solution.py:824
